TPU v7x, 128 devices: a whole 4x4x4 slice. The times are simulated.
128 devices in a mesh: space: 32 (over y, x, core), dirs: 4 (over z).
Axes of the slice: x: 4, y: 4, z: 4, core: 2. Of those that a mesh axis runs over, the one named last changes fastest.
Arguments:
- history: bfloat16 [32, 32, 32768], P(None, None, 'space'), may hold values from -6 to 6
- radiation: bfloat16 [4, 32768, 2048], P(None, 'space'), may hold values from -0.125 to 0.125
- near_matrix: bfloat16 [256, 8, 128, 128], P('space'), may hold values from -0.1875 to 0.1875
- near_offset: int32 [256, 8], P('space'), may hold values from -4 to 4
- near_delay: int32 [256, 8], P('space'), may hold values from 0 to 31
- far_source: int32 [64, 8], replicated, may hold values from 0 to 63
- far_delay: int32 [64, 8], replicated, may hold values from 0 to 16
- far_weight: bfloat16 [64, 8, 2048], P('space', None, 'dirs'), may hold values from -2 to 2
Outputs:
- near_field: bfloat16 [32, 32768], P('dirs', 'space')
- far_field: bfloat16 [32, 32, 32768], P(None, 'dirs', 'space')
Inputs may be any that keep to these rules, and one draw needn't show every extreme that they name: `near_offset`: sources outside the 256 blocks contribute nothing. `far_source`: a group may appear in many lists and twice in one.
All inputs are finite; a program needn't handle non-finite values.
Results may differ from a plain program's by a relative error of at most 0.0058.
Values may be sent and summed in bfloat16 or wider, within the bound.
A program may use at most 256 MiB of HBM per device.

v0:
```python
import jax
import jax.numpy as jnp
from jax import lax
from jax.sharding import PartitionSpec as P

GRP_BLK = 4
HB = 4


def extended_2(array, sides, width):
    for axis, dim in sides:
        count, length = (lax.axis_size(axis), array.shape[dim])
        up = [(i, (i + 1) % count) for i in range(count - 1)]
        down = [(j, i) for i, j in up]
        last = lax.slice_in_dim(array, length - width, length, axis=dim)
        initial = lax.slice_in_dim(array, 0, width, axis=dim)
        before = lax.ppermute(last, axis, up)
        after = lax.ppermute(initial, axis, down)
        array = jnp.concatenate([before, array, after], axis=dim)
    return array


def translate(table, weights, far_source, far_delay):
    grp_count = table.shape[0]
    tap_count = table.shape[1]
    span = tap_count + tap_count // 2
    padded = jnp.concatenate(
        [table, jnp.zeros((grp_count, tap_count // 2) + table.shape[2:], table.dtype)], axis=1
    )
    flat_table = padded.reshape((grp_count * span,) + table.shape[2:])
    tap_ids = jnp.arange(tap_count, dtype=jnp.int32)[None, :]
    summed = jnp.zeros(table.shape, jnp.float32)
    for slot_idx in range(far_source.shape[1]):
        row_ids = (
            far_source[:, slot_idx][:, None] * span + tap_ids + far_delay[:, slot_idx][:, None]
        )
        arrived = jnp.take(flat_table, row_ids.reshape(-1), axis=0).reshape(table.shape)
        summed = summed + weights[:, slot_idx][:, None].astype(jnp.float32) * arrived.astype(
            jnp.float32
        )
    return summed.astype(jnp.bfloat16)


def local(
    history, radiation, near_matrix, near_offset, near_delay, far_source, far_delay, far_weight
):
    tap_count, exc_count, cur_count = history.shape
    quad_count = radiation.shape[0]
    full_dirs = radiation.shape[2]
    blk_count, slot_count, width, _ = near_matrix.shape
    grp_count = blk_count // GRP_BLK
    grp_width = cur_count // grp_count
    dirs_size = lax.axis_size("dirs")
    dir_part = full_dirs // dirs_size
    exc_part = exc_count // dirs_size
    own_hist = lax.dynamic_slice_in_dim(history, lax.axis_index("dirs") * exc_part, exc_part, 1)
    extended = extended_2(own_hist, (("space", 2),), HB * width)
    extended = extended.reshape(tap_count, exc_part, blk_count + 2 * HB, width)
    src_blocks = jnp.arange(blk_count, dtype=jnp.int32)[:, None] + HB + near_offset
    sources = extended[near_delay, :, src_blocks]
    near_sum = jnp.einsum(
        "isen,ismn->eim", sources, near_matrix, preferred_element_type=jnp.float32
    )
    near_field = near_sum.reshape(exc_part, cur_count).astype(jnp.bfloat16)
    own_rad = lax.dynamic_slice_in_dim(radiation, lax.axis_index("dirs") * dir_part, dir_part, 2)
    hist_groups = history.reshape(tap_count, exc_count, grp_count, grp_width)
    zero_tail = jnp.zeros((quad_count - 1, exc_count, grp_count, grp_width), history.dtype)
    padded = jnp.concatenate([hist_groups, zero_tail], axis=0)
    agg_groups = own_rad.reshape(quad_count, grp_count, grp_width, dir_part)
    summed = jnp.zeros((grp_count, tap_count, exc_count, dir_part), jnp.float32)
    for tap_idx in range(quad_count):
        summed = summed + jnp.einsum(
            "aegn,gnk->gaek",
            padded[tap_idx : tap_idx + tap_count],
            agg_groups[tap_idx],
            preferred_element_type=jnp.float32,
        )
    ray_tiles = summed.astype(jnp.bfloat16)
    arrived = lax.all_to_all(ray_tiles, "space", split_axis=2, concat_axis=0, tiled=True)
    all_weights = lax.all_gather(far_weight, "space", axis=0, tiled=True)
    slot_weights = all_weights[:, :, None, :]
    translated = translate(arrived, slot_weights, far_source, far_delay)
    incoming = lax.all_to_all(translated, "space", split_axis=0, concat_axis=2, tiled=True)
    zero_head = jnp.zeros((grp_count, quad_count - 1, exc_count, dir_part), jnp.bfloat16)
    delayed_in = jnp.concatenate([zero_head, incoming], axis=1)
    projected = jnp.zeros(
        (lax.axis_size("dirs") * exc_part, tap_count, grp_count, grp_width), jnp.float32
    )
    for tap_idx in range(quad_count):
        first_row = quad_count - 1 - tap_idx
        projected = projected + jnp.einsum(
            "gaek,gnk->eagn",
            delayed_in[:, first_row : first_row + tap_count],
            agg_groups[tap_idx],
            preferred_element_type=jnp.float32,
        )
    far_sum = lax.psum_scatter(
        projected.reshape(lax.axis_size("dirs") * exc_part, tap_count, cur_count),
        "dirs",
        scatter_dimension=0,
        tiled=True,
    )
    far_field = far_sum.transpose(1, 0, 2).astype(jnp.bfloat16)
    return (near_field, far_field)


def solution(mesh):
    in_specs = (
        P(None, None, "space"),
        P(None, "space", None),
        P("space", None, None, None),
        P("space", None),
        P("space", None),
        P(),
        P(),
        P("space", None, "dirs"),
    )
    out_specs = (P("dirs", "space"), P(None, "dirs", "space"))
    return jax.shard_map(local, mesh=mesh, in_specs=in_specs, out_specs=out_specs, check_vma=False)
```

profile of v0, /device:TPU:1, one launch (start us, length us, event | category | flops | bytes accessed | tf_op | source)
XLA Modules:
  0.0 300.5 jit_solution(12961721396351592757)
XLA Ops:
  7.2 3.4 %copy.58 = bf16[32,4,2,8,512]{4,3,1,0,2:T(8,128)(2,1)} copy(bf16[32,4,2,8,512]{4,3,2,1,0:T(8,128)(2,1)} %bitcast.197) | data formatting | bytes 4194304 | tf_op jit(solution)/shard_map/reshape | solution.py:66
  10.6 2.6 constant_dynamic-slice_fusion.1
  13.5 1.2 fusion.35
  14.8 1.2 fusion.36
  16.3 1.2 fusion.37
  17.6 1.3 add_convert_fusion
  18.9 2.5 copy.18
  21.4 8.8 %all-to-all-start = ((bf16[2,32,32,512]{3,1,0,2:T(8,128)(2,1)}), bf16[2,32,32,512]{3,1,0,2:T(8,128)(2,1)}, u32[]{:S(2)}, u32[]{:S(2)}) async-start(bf16[2,32,32,512]{3,1,0,2:T(8,128)(2,1)} %copy.18), calls=%async_computation | async-start | bytes 4194304 | tf_op jit(solution)/shard_map/all_to_all | solution.py:79
  30.5 0.6 compare_and_fusion.5
  31.2 0.6 compare_and_fusion.4
  31.9 0.6 fusion.23
  32.6 0.6 compare_and_fusion.3
  33.2 0.6 fusion.24
  33.8 0.6 compare_and_fusion.2
  34.6 0.6 fusion.25
  35.2 0.6 compare_and_fusion.1
  36.0 0.6 compare_and_fusion.7
  36.6 0.6 compare_and_fusion.6
  37.3 0.6 compare_and_fusion
  37.9 37.0 %all_gather.3 = bf16[64,8,512]{2,1,0:T(8,128)(2,1)S(1)} all-gather(bf16[2,8,512]{2,1,0:T(8,128)(2,1)S(1)} %copy-done.27), channel_id=1, replica_groups=mesh['space'=32,'dirs'=4] {'space'}, dimensions={0}, use_global_device_ids=true | all-gather | bytes 540672 | tf_op jit(solution)/shard_map/all_gather | solution.py:80
  74.9 0.6 fusion.19
  75.5 0.6 fusion.20
  76.1 0.6 fusion.26
  76.7 0.7 slice_convert_fusion.7
  77.4 0.7 copy_bitcast_fusion.4
  78.1 0.7 copy_bitcast_fusion.6
  78.8 0.7 copy_bitcast_fusion.8
  79.5 3.6 %concatenate.18 = bf16[64,48,1,512]{3,1,0,2:T(8,128)(2,1)} pad(bf16[64,32,1,512]{3,1,0,2:T(8,128)(2,1)} %bitcast.27, bf16[]{:T(256)} %constant.6.clone.1), padding=0_0x0_16x0_0x0_0 | pad | bytes 5242882 | tf_op jit(solution)/shard_map/concatenate | solution.py:27
  83.2 11.7 %gather_fusion.3 = bf16[2048,512]{1,0:T(8,128)(2,1)} fusion(bf16[3072,512]{1,0:T(8,128)(2,1)} %bitcast.189, s32[2048]{0:T(1024)S(1)} %fusion.21), kind=kCustom, calls=%fused_computation.2.clone | custom fusion | bytes 4202496 | tf_op jit(solution)/shard_map/jit(_take)/gather | solution.py:37
  94.8 11.5 %gather_fusion.4 = bf16[2048,512]{1,0:T(8,128)(2,1)} fusion(bf16[3072,512]{1,0:T(8,128)(2,1)} %bitcast.190, s32[2048]{0:T(1024)S(1)} %fusion.22), kind=kCustom, calls=%fused_computation.3.clone | custom fusion | bytes 4202496 | tf_op jit(solution)/shard_map/jit(_take)/gather | solution.py:37
  106.4 11.5 %gather_fusion.5 = bf16[2048,512]{1,0:T(8,128)(2,1)} fusion(bf16[3072,512]{1,0:T(8,128)(2,1)} %bitcast.191, s32[2048]{0:T(1024)S(1)} %copy-done.21), kind=kCustom, calls=%fused_computation.4.clone | custom fusion | bytes 4202496 | tf_op jit(solution)/shard_map/jit(_take)/gather | solution.py:37
  117.9 11.6 %gather_fusion.6 = bf16[2048,512]{1,0:T(8,128)(2,1)} fusion(bf16[3072,512]{1,0:T(8,128)(2,1)} %bitcast.192, s32[2048]{0:T(1024)S(1)} %copy-done.22), kind=kCustom, calls=%fused_computation.5.clone | custom fusion | bytes 4202496 | tf_op jit(solution)/shard_map/jit(_take)/gather | solution.py:37
  129.5 11.5 %gather_fusion.7 = bf16[2048,512]{1,0:T(8,128)(2,1)} fusion(bf16[3072,512]{1,0:T(8,128)(2,1)} %bitcast.193, s32[2048]{0:T(1024)S(1)} %copy-done.23), kind=kCustom, calls=%fused_computation.6.clone | custom fusion | bytes 4202496 | tf_op jit(solution)/shard_map/jit(_take)/gather | solution.py:37
  141.0 11.5 %gather_fusion.1 = bf16[2048,512]{1,0:T(8,128)(2,1)} fusion(bf16[3072,512]{1,0:T(8,128)(2,1)} %bitcast.194, s32[2048]{0:T(1024)S(1)} %copy-done.24), kind=kCustom, calls=%fused_computation.clone | custom fusion | bytes 4202496 | tf_op jit(solution)/shard_map/jit(_take)/gather | solution.py:37
  152.5 11.5 %gather_fusion.2 = bf16[2048,512]{1,0:T(8,128)(2,1)} fusion(bf16[3072,512]{1,0:T(8,128)(2,1)} %bitcast.195, s32[2048]{0:T(1024)S(1)} %copy-done.25), kind=kCustom, calls=%fused_computation.1.clone | custom fusion | bytes 4202496 | tf_op jit(solution)/shard_map/jit(_take)/gather | solution.py:37
  164.1 11.5 %gather_fusion.8 = bf16[2048,512]{1,0:T(8,128)(2,1)} fusion(bf16[3072,512]{1,0:T(8,128)(2,1)} %bitcast.196, s32[2048]{0:T(1024)S(1)} %copy-done.26), kind=kCustom, calls=%fused_computation.7.clone | custom fusion | bytes 4202496 | tf_op jit(solution)/shard_map/jit(_take)/gather | solution.py:37
  175.6 1.9 bitcast_select_fusion.5
  178.2 1.1 copy-done.14
  179.8 1.1 copy-done.13
  181.4 1.1 copy-done.12
  183.0 1.1 copy-done.11
  184.6 1.1 copy-done.10
  186.2 1.1 copy-done.9
  187.4 0.5 bitcast_select_fusion
  188.5 4.6 %fusion.1 = bf16[64,32,1,512]{3,1,2,0:T(8,128)(2,1)S(1)} fusion(bf16[64,32,1,512]{3,1,2,0:T(8,128)(2,1)S(1)} %bitcast.223, bf16[64,32,1,512]{3,1,2,0:T(8,128)(2,1)S(1)} %bitcast.220, bf16[64,32,1,512]{3,1,2,0:T(8,128)(2,1)S(1)} %bitcast.219, bf16[64,32,1,512]{3,1,2,0:T(8,128)(2,1)S(1)} %bitcast.218, bf16[64,32,1,512]{3,1,2,0:T(8,128)(2,1)S(1)} %bitcast.217, ...), kind=kLoop, calls=%fused_computation.11 | loop fusion | flops 25165824 | bytes 19922944 | tf_op jit(solution)/shard_map/convert_element_type | solution.py:41
  193.1 33.3 %all_to_all.36 = bf16[64,32,1,512]{3,1,2,0:T(8,128)(2,1)S(1)} all-to-all(bf16[64,32,1,512]{3,1,2,0:T(8,128)(2,1)S(1)} %fusion.1), channel_id=1, replica_groups=mesh['space'=32,'dirs'=4] {'space'}, dimensions={0} | all-to-all | bytes 4194304 | tf_op jit(solution)/shard_map/all_to_all | solution.py:83
  226.4 1.2 copy.59
  227.7 1.3 fusion.12
  229.0 1.3 fusion.10
  230.3 1.3 fusion.8
  231.5 2.2 add_bitcast_fusion
  233.7 5.2 %copy.28 = f32[32,32,2,512]{3,2,1,0:T(2,128)} copy(f32[32,32,2,512]{3,0,1,2:T(8,128)S(1)} %add_bitcast_fusion) | data formatting | bytes 8388608 | tf_op jit(solution)/shard_map/add | solution.py:91
  239.0 6.6 %reshape.321 = f32[32,32,1024]{2,1,0:T(8,128)} reshape(f32[32,32,2,512]{3,2,1,0:T(2,128)} %copy.28) | data formatting | bytes 8388608 | tf_op jit(solution)/shard_map/reshape | solution.py:98
  245.6 1.1 constant_dynamic-slice_fusion.4
  246.7 2.5 collective-permute-start
  249.2 2.5 collective-permute-start.1
  251.9 1.1 constant_dynamic-slice_fusion.6
  253.0 4.3 %collective-permute-done.1 = bf16[32,8,512]{2,1,0:T(8,128)(2,1)} collective-permute-done((bf16[32,8,512]{2,1,0:T(8,128)(2,1)S(1)}, bf16[32,8,512]{2,1,0:T(8,128)(2,1)}, u32[]{:S(2)}, u32[]{:S(2)}) %collective-permute-start.1) | collective-permute-done | bytes 262176 | tf_op jit(solution)/shard_map/ppermute | solution.py:18
  257.3 2.1 maximum_bitcast_fusion
  259.4 2.0 gather_fusion
  261.4 1.3 fusion.18
  262.7 28.6 %reduce-scatter.2.cloned.1.call-done = f32[8,32,1024]{2,1,0:T(8,128)} async-done(((f32[32,32,1024]{2,1,0:T(8,128)}), f32[8,32,1024]{2,1,0:T(8,128)}) %reduce-scatter.2.cloned.1.call-update) | async-done | bytes 1048592 | tf_op jit(solution)/shard_map/reduce_scatter | solution.py:97
  291.2 1.3 convert_bitcast_fusion
  292.5 1.1 copy.29
  (104 shorter events, 5.5 us)
Async XLA Ops:
  7.2 254.2 %copy-start = (bf16[8,8,128,128]{3,2,1,0:T(8,128)(2,1)S(1)}, bf16[8,8,128,128]{3,2,1,0:T(8,128)(2,1)}, u32[]{:S(2)}) copy-start(bf16[8,8,128,128]{3,2,1,0:T(8,128)(2,1)} %param.12) | copy-start | bytes 6291460
  10.6 2.9 copy-start.1
  13.2 1.5 copy-start.4
  13.2 1.5 copy-start.6
  13.2 4.4 %copy-start.2 = (bf16[1,1024,512]{2,1,0:T(8,128)(2,1)}, bf16[1,1024,512]{2,1,0:T(8,128)(2,1)S(1)}, u32[]{:S(2)}) copy-start(bf16[1,1024,512]{2,1,0:T(8,128)(2,1)S(1)} %get-tuple-element.10) | copy-start | bytes 3145732
  14.7 1.6 copy-start.8
  21.4 8.9 %copy-start.38 = (s32[64,8]{0,1:T(8,128)S(1)}, s32[64,8]{0,1:T(8,128)}, u32[]{:S(2)}) copy-start(s32[64,8]{0,1:T(8,128)} %param.15) | copy-start | bytes 6148
  21.4 8.9 %copy-start.39 = (s32[64,8]{0,1:T(8,128)S(1)}, s32[64,8]{0,1:T(8,128)}, u32[]{:S(2)}) copy-start(s32[64,8]{0,1:T(8,128)} %param.16) | copy-start | bytes 6148
  21.4 16.5 %copy-start.27 = (bf16[2,8,512]{2,1,0:T(8,128)(2,1)S(1)}, bf16[2,8,512]{2,1,0:T(8,128)(2,1)}, u32[]{:S(2)}) copy-start(bf16[2,8,512]{2,1,0:T(8,128)(2,1)} %param.17) | copy-start | bytes 49156
  21.4 58.1 %all-to-all-start = ((bf16[2,32,32,512]{3,1,0,2:T(8,128)(2,1)}), bf16[2,32,32,512]{3,1,0,2:T(8,128)(2,1)}, u32[]{:S(2)}, u32[]{:S(2)}) async-start(bf16[2,32,32,512]{3,1,0,2:T(8,128)(2,1)} %copy.18), calls=%async_computation | async-start | bytes 4194304 | tf_op jit(solution)/shard_map/all_to_all | solution.py:79
  30.2 261.0 %reduce-scatter.2.cloned.1.call-start = ((), (), s32[]{:S(2)}) async-start(), calls=%async_computation.3 | async-start | bytes 5242880 | tf_op jit(solution)/shard_map/reduce_scatter | solution.py:97
  94.8 11.5 %copy-start.21 = (s32[2048]{0:T(1024)S(1)}, s32[2048]{0:T(1024)}, u32[]{:S(2)}) copy-start(s32[2048]{0:T(1024)} %fusion.23) | copy-start | bytes 24580
  106.4 11.5 %copy-start.22 = (s32[2048]{0:T(1024)S(1)}, s32[2048]{0:T(1024)}, u32[]{:S(2)}) copy-start(s32[2048]{0:T(1024)} %fusion.24) | copy-start | bytes 24580
  117.9 11.6 %copy-start.23 = (s32[2048]{0:T(1024)S(1)}, s32[2048]{0:T(1024)}, u32[]{:S(2)}) copy-start(s32[2048]{0:T(1024)} %fusion.25) | copy-start | bytes 24580
  129.5 11.5 %copy-start.24 = (s32[2048]{0:T(1024)S(1)}, s32[2048]{0:T(1024)}, u32[]{:S(2)}) copy-start(s32[2048]{0:T(1024)} %fusion.19) | copy-start | bytes 24580
  141.0 11.5 %copy-start.25 = (s32[2048]{0:T(1024)S(1)}, s32[2048]{0:T(1024)}, u32[]{:S(2)}) copy-start(s32[2048]{0:T(1024)} %fusion.20) | copy-start | bytes 24580
  152.5 11.5 %copy-start.26 = (s32[2048]{0:T(1024)S(1)}, s32[2048]{0:T(1024)}, u32[]{:S(2)}) copy-start(s32[2048]{0:T(1024)} %fusion.26) | copy-start | bytes 24580
  164.1 11.5 %copy-start.28 = (pred[2048]{0:T(1024)(128)(4,1)S(1)}, pred[2048]{0:T(1024)(128)(4,1)}, u32[]{:S(2)}) copy-start(pred[2048]{0:T(1024)(128)(4,1)} %compare_and_fusion.5) | copy-start | bytes 6148
  175.6 2.2 copy-start.15
  175.6 2.2 copy-start.29
  177.8 1.6 copy-start.14
  177.8 1.6 copy-start.30
  179.4 1.6 copy-start.13
  179.4 1.6 copy-start.31
  181.0 1.6 copy-start.12
  181.0 1.6 copy-start.32
  182.6 1.6 copy-start.11
  182.6 1.6 copy-start.33
  184.2 1.6 copy-start.10
  184.2 1.6 copy-start.34
  185.8 1.6 copy-start.9
  185.8 1.6 copy-start.35
  187.4 0.9 copy-start.16
  187.4 1.0 copy-start.17
  187.4 1.0 copy-start.18
  187.4 1.1 copy-start.19
  187.4 1.1 copy-start.20
  226.4 1.2 copy-start.7
  227.7 1.3 copy-start.5
  228.9 1.3 copy-start.3
  245.6 6.1 %copy-start.36 = (s32[8,8]{1,0:T(8,128)S(1)}, s32[8,8]{1,0:T(8,128)}, u32[]{:S(2)}) copy-start(s32[8,8]{1,0:T(8,128)} %param.14) | copy-start | bytes 772
  245.6 6.1 %copy-start.37 = (s32[8,8]{1,0:T(8,128)S(1)}, s32[8,8]{1,0:T(8,128)}, u32[]{:S(2)}) copy-start(s32[8,8]{1,0:T(8,128)} %param.13) | copy-start | bytes 772
  246.7 6.3 %collective-permute-start = (bf16[32,8,512]{2,1,0:T(8,128)(2,1)S(1)}, bf16[32,8,512]{2,1,0:T(8,128)(2,1)}, u32[]{:S(2)}, u32[]{:S(2)}) collective-permute-start(bf16[32,8,512]{2,1,0:T(8,128)(2,1)S(1)} %get-tuple-element.11), channel_id=1, source_target_pairs={{0,4},{4,8},{8,12},{12,16},{16,20},{20,24},{24,28},{28,32},{32,36}... | collective-permute-start | bytes 786440 | tf_op jit(solution)/shard_map/ppermute | solution.py:17
  249.2 8.1 %collective-permute-start.1 = (bf16[32,8,512]{2,1,0:T(8,128)(2,1)S(1)}, bf16[32,8,512]{2,1,0:T(8,128)(2,1)}, u32[]{:S(2)}, u32[]{:S(2)}) collective-permute-start(bf16[32,8,512]{2,1,0:T(8,128)(2,1)S(1)} %get-tuple-element.12), channel_id=1, source_target_pairs={{4,0},{8,4},{12,8},{16,12},{20,16},{24,20},{28,24},{32,28},{36,32}... | collective-permute-start | bytes 786440 | tf_op jit(solution)/shard_map/ppermute | solution.py:18
Sparse Core Ops, SparseCore 0:
  245.7 45.4 reduce-scatter.1
where the time goes:
time: 302 us; the launch traced here: 300 us
  local copies, waits for them, and re-layouts  134 us (44%)
  blocking collectives  70.3 us (23%)
  waiting for transfers between devices  32.8 us (11%)
  other arithmetic  22.5 us (7%)
  between operations  14.5 us (5%)
  starting transfers between devices  13.8 us (5%)
  matrix products  12.4 us (4%)
    gather x8, local copies, waits for them, and re-layouts, translate(): jnp.take(flat_table, row_ids.reshape(-1), axis=0).reshape(table.shape)  92.4 us
    all_gather x1, blocking collectives, local(): all_weights = lax.all_gather(far_weight, 'space', axis=0, tiled=True)  37 us
    all_to_all x1, blocking collectives, local(): lax.all_to_all(translated, 'space', split_axis=0, concat_axis=2, tiled=True)  33.3 us
    reduce_scatter x1, waiting for transfers between devices, local(): lax.psum_scatter(projected.reshape(lax.axis_size('dirs') * exc_part, tap_...  28.6 us
    unnamed x85, local copies, waits for them, and re-layouts  11.8 us
    all_to_all x1, starting transfers between devices, local(): lax.all_to_all(ray_tiles, 'space', split_axis=2, concat_axis=0, tiled=True)  8.79 us
    reshape x1, local copies, waits for them, and re-layouts, local(): projected.reshape(lax.axis_size('dirs') * exc_part, tap_count, cur_count)  6.6 us
    dot_general x4, matrix products, local(): jnp.einsum('gaek,gnk->eagn', delayed_in[:, first_row:first_row + tap_coun...  6.04 us
  transfers between devices with their start and end apart: 4, of which 2 were waited for; matrix products, arithmetic and copies ran while one was open for 7% of the time, Pallas kernels for 0%

commit v1 on v0

v1 whole, which is shorter than its diff:
```python
import functools

import jax
import jax.numpy as jnp
from jax import lax
from jax.experimental import pallas as pl
from jax.experimental.pallas import tpu as pltpu
from jax.sharding import PartitionSpec as P

MESH = pl.DeviceIdType.MESH
LANES = 128
TAPS = 32
QT = 4
LIST = 8
NEAR = 8
BLK = 8
HB = 4
EXC = 8
HALF = EXC // 2
ROWS = TAPS * HALF
SPAN = ROWS + 16 * HALF
GRP = 512
MSG = 2 * ROWS + 2 * LIST


def kernel(
    n_space,
    n_dirs,
    hq_ref,
    hb_ref,
    rad_ref,
    mat_ref,
    w_ref,
    off_ref,
    del_ref,
    src_ref,
    lag_ref,
    far_ref,
    near_ref,
    hq,
    hb,
    halo,
    ext,
    mat,
    rad,
    wz,
    send1,
    recv1,
    table,
    wtab,
    send2,
    recv2,
    padded,
    acc,
    hq_sem,
    rad_sem,
    mat_sem,
    w_sem,
    z_send,
    z_recv,
    halo_send,
    halo_recv,
    own_sem,
    send1_sem,
    recv1_sem,
    send2_sem,
    recv2_sem,
):
    n_pair = n_space // 4
    per_plane = w_ref.shape[0]
    me = lax.axis_index("space")
    plane = lax.axis_index("dirs")
    my_pair = lax.div(me, 4)
    right, left = lax.rem(me + 1, n_space), lax.rem(me + n_space - 1, n_space)

    def pair_at(i):
        return lax.rem(my_pair + i, n_pair)

    def pair_from(i):
        return lax.rem(my_pair + n_pair - i, n_pair)

    def rad_copy(p, g):
        cols = pl.ds(pl.multiple_of(p * 256, 256), 256)
        return pltpu.make_async_copy(rad_ref.at[:, g, :, cols], rad.at[p, g], rad_sem.at[p, g])

    def z_copy(to):
        return pltpu.make_async_remote_copy(
            src_ref=wz.at[plane],
            dst_ref=wz.at[plane],
            send_sem=z_send.at[to],
            recv_sem=z_recv.at[plane],
            device_id={"dirs": to},
            device_id_type=MESH,
        )

    def z_arrival(frm):
        return pltpu.make_async_remote_copy(
            src_ref=wz.at[frm],
            dst_ref=wz.at[frm],
            send_sem=z_send.at[frm],
            recv_sem=z_recv.at[frm],
            device_id={"dirs": frm},
            device_id_type=MESH,
        )

    def to_translator(t, slot):
        return pltpu.make_async_remote_copy(
            src_ref=send1.at[t],
            dst_ref=recv1.at[slot],
            send_sem=send1_sem.at[t],
            recv_sem=recv1_sem.at[slot],
            device_id={"space": t},
            device_id_type=MESH,
        )

    def to_owner(t, slot):
        return pltpu.make_async_remote_copy(
            src_ref=send2.at[t],
            dst_ref=recv2.at[slot],
            send_sem=send2_sem.at[t],
            recv_sem=recv2_sem.at[slot],
            device_id={"space": t},
            device_id_type=MESH,
        )

    def halo_copy(side):
        return pltpu.make_async_remote_copy(
            src_ref=hb.at[pl.ds(BLK - HB if side == 0 else 0, HB)],
            dst_ref=halo.at[side],
            send_sem=halo_send.at[side],
            recv_sem=halo_recv.at[side],
            device_id={"space": right if side == 0 else left},
            device_id_type=MESH,
        )

    hq_copy = pltpu.make_async_copy(hq_ref, hq, hq_sem.at[0])
    hb_copy = pltpu.make_async_copy(hb_ref, hb, hq_sem.at[1])
    mat_copy = pltpu.make_async_copy(mat_ref, mat, mat_sem)
    w_copy = pltpu.make_async_copy(w_ref, wz.at[plane], w_sem)

    barrier = pltpu.get_barrier_semaphore()

    def greet(i, carry):
        pl.semaphore_signal(
            barrier, inc=1, device_id={"space": lax.rem(me + i, n_space)}, device_id_type=MESH
        )
        return carry

    lax.fori_loop(1, n_space, greet, 0)
    for i in range(1, n_dirs):
        pl.semaphore_signal(
            barrier, inc=1, device_id={"dirs": lax.rem(plane + i, n_dirs)}, device_id_type=MESH
        )

    w_copy.start()
    hq_copy.start()

    def fetch(i, carry):
        for g in range(2):
            rad_copy(pair_at(i), g).start()
        return carry

    lax.fori_loop(0, n_pair, fetch, 0)
    hb_copy.start()
    mat_copy.start()
    w_copy.wait()
    pl.semaphore_wait(barrier, n_space - 1 + n_dirs - 1)
    for i in range(1, n_dirs):
        z_copy(lax.rem(plane + i, n_dirs)).start()
    hq_copy.wait()

    def aggregate(p):
        for g in range(2):
            rad_copy(p, g).wait()
            rays = jnp.dot(
                hq[g],
                rad[p, g].reshape(QT * GRP, 256),
                preferred_element_type=jnp.float32,
            ).astype(jnp.bfloat16)
            for jj in range(2):
                for c in range(2):
                    send1[4 * p + 2 * jj + c, pl.ds(g * ROWS, ROWS), :] = rays[
                        c * ROWS : (c + 1) * ROWS, jj * LANES : (jj + 1) * LANES
                    ]

    def dispatch(p):
        for jj in range(2):
            chip = 2 * p + jj
            weights = wz[lax.div(chip, per_plane), lax.rem(chip, per_plane)]
            for c in range(2):
                t = 4 * p + 2 * jj + c
                send1[t, pl.ds(2 * ROWS, 2 * LIST), :] = weights

                @pl.when(t != me)
                def _():
                    to_translator(t, me).start()

                @pl.when(t == me)
                def _():
                    pltpu.make_async_copy(send1.at[t], recv1.at[t], own_sem).start()

    aggregate(my_pair)
    for i in range(1, n_dirs):
        z_arrival(lax.rem(plane + n_dirs - i, n_dirs)).wait_recv()
    dispatch(my_pair)

    def agg_step(i, carry):
        p = pair_at(i)
        aggregate(p)
        dispatch(p)
        return carry

    lax.fori_loop(1, n_pair, agg_step, 0)

    hb_copy.wait()
    halo_copy(0).start()
    halo_copy(1).start()

    table[:, ROWS:SPAN, :] = jnp.zeros((table.shape[0], SPAN - ROWS, LANES), jnp.float32)
    acc[...] = jnp.zeros_like(acc)
    padded[:, :, 0:16, :] = jnp.zeros((2, 2, 16, 256), jnp.bfloat16)

    def own_blocks(b, carry):
        ext[HB + b] = hb[b].astype(jnp.float32).reshape(TAPS, EXC, LANES)
        return carry

    lax.fori_loop(0, BLK, own_blocks, 0)

    def take_in(i, carry):
        p = pair_from(i)
        for j in range(4):
            s = 4 * p + j

            @pl.when(s != me)
            def _():
                to_translator(s, s).wait_recv()

            @pl.when(s == me)
            def _():
                pltpu.make_async_copy(send1.at[s], recv1.at[s], own_sem).wait()

            for g in range(2):
                table[2 * s + g, 0:ROWS, :] = recv1[s, g * ROWS : (g + 1) * ROWS, :].astype(
                    jnp.float32
                )
            wtab[s] = recv1[s, 2 * ROWS : MSG, :].astype(jnp.float32)
        return carry

    lax.fori_loop(0, n_pair, take_in, 0)

    def translate(i, carry):
        p = pair_at(i)
        for j in range(4):
            t = 4 * p + j
            for g in range(2):
                weights = wtab[t, g * LIST : (g + 1) * LIST, :]
                total = jnp.zeros((ROWS, LANES), jnp.float32)
                for slot in range(LIST):
                    entry = (2 * t + g) * LIST + slot
                    first = lag_ref[entry] * HALF
                    total = (
                        total
                        + weights[slot : slot + 1, :] * table[src_ref[entry], pl.ds(first, ROWS), :]
                    )
                send2[t, g * ROWS : (g + 1) * ROWS, :] = total.astype(jnp.bfloat16)

            @pl.when(t != me)
            def _():
                to_owner(t, me).start()

            @pl.when(t == me)
            def _():
                pltpu.make_async_copy(send2.at[t], recv2.at[t], own_sem).start()

        return carry

    lax.fori_loop(0, n_pair, translate, 0)

    for side in range(2):
        halo_copy(side).wait_recv()

    def halo_blocks(b, carry):
        ext[b] = halo[0, b].astype(jnp.float32).reshape(TAPS, EXC, LANES)
        ext[HB + BLK + b] = halo[1, b].astype(jnp.float32).reshape(TAPS, EXC, LANES)
        return carry

    lax.fori_loop(0, HB, halo_blocks, 0)
    mat_copy.wait()

    for b in range(BLK):
        near = jnp.zeros((EXC, LANES), jnp.float32)
        for slot in range(NEAR):
            shift = off_ref[b * NEAR + slot]
            block = me * BLK + b + shift
            inside = jnp.logical_and(block >= 0, block < n_space * BLK)
            values = ext[b + HB + shift, del_ref[b * NEAR + slot]]
            values = jnp.where(inside, values, 0.0).astype(jnp.bfloat16)
            near = near + lax.dot_general(
                values,
                mat[b, slot],
                (((1,), (1,)), ((), ())),
                preferred_element_type=jnp.float32,
            )
        near_ref[:, b * LANES : (b + 1) * LANES] = near.astype(jnp.bfloat16)

    def project(i, carry):
        p = pair_from(i)
        for j in range(4):
            s = 4 * p + j

            @pl.when(s != me)
            def _():
                to_owner(s, s).wait_recv()

            @pl.when(s == me)
            def _():
                pltpu.make_async_copy(send2.at[s], recv2.at[s], own_sem).wait()

            jj, c = j // 2, j % 2
            for g in range(2):
                padded[g, c, 16 : 16 + ROWS, jj * LANES : (jj + 1) * LANES] = recv2[
                    s, g * ROWS : (g + 1) * ROWS, :
                ]
        for g in range(2):
            total = acc[g]
            for q in range(QT):
                start = 16 - q * HALF
                late = jnp.concatenate(
                    [padded[g, c, start : start + ROWS, :] for c in range(2)], axis=0
                )
                total = total + lax.dot_general(
                    late,
                    rad[p, g, q],
                    (((1,), (1,)), ((), ())),
                    preferred_element_type=jnp.float32,
                )
            acc[g] = total
        return carry

    lax.fori_loop(0, n_pair, project, 0)
    for g in range(2):
        far_ref[:, g * GRP : (g + 1) * GRP] = acc[g].astype(jnp.bfloat16)

    def drain(i, carry):
        t = lax.rem(me + i, n_space)
        to_translator(t, me).wait_send()
        to_owner(t, me).wait_send()
        return carry

    lax.fori_loop(1, n_space, drain, 0)
    for i in range(1, n_dirs):
        z_copy(lax.rem(plane + i, n_dirs)).wait_send()
    for side in range(2):
        halo_copy(side).wait_send()


def local(
    n_space,
    n_dirs,
    history,
    radiation,
    near_matrix,
    near_offset,
    near_delay,
    far_source,
    far_delay,
    far_weight,
):
    cur = history.shape[2]
    dirs = radiation.shape[2]
    own = lax.dynamic_slice_in_dim(history, lax.axis_index("dirs") * EXC, EXC, 1)
    blocks = own.reshape(TAPS * EXC, BLK, LANES).transpose(1, 0, 2)
    rows = own.reshape(TAPS, 2, HALF, cur).transpose(1, 0, 2, 3)
    late = jnp.concatenate([rows, jnp.zeros((2, QT - 1, HALF, cur), rows.dtype)], axis=1)
    stacked = jnp.stack(
        [late[:, q : q + TAPS].reshape(2 * ROWS, 2, GRP) for q in range(QT)], axis=2
    )
    hq = stacked.transpose(1, 0, 2, 3).reshape(2, 2 * ROWS, QT * GRP)
    weights = far_weight.reshape(2 * LIST, -1, LANES).transpose(1, 0, 2)
    n_pair = n_space // 4
    any_spec = pl.BlockSpec(memory_space=pl.ANY)
    smem = pl.BlockSpec(memory_space=pltpu.SMEM)
    vmem = pl.BlockSpec(memory_space=pltpu.VMEM)
    bf16, f32 = jnp.bfloat16, jnp.float32
    far, near = pl.pallas_call(
        functools.partial(kernel, n_space, n_dirs),
        out_shape=(
            jax.ShapeDtypeStruct((2 * ROWS, cur), bf16),
            jax.ShapeDtypeStruct((EXC, cur), bf16),
        ),
        in_specs=[any_spec] * 5 + [smem] * 4,
        out_specs=(vmem, vmem),
        scratch_shapes=[
            pltpu.VMEM((2, 2 * ROWS, QT * GRP), bf16),
            pltpu.VMEM((BLK, TAPS * EXC, LANES), bf16),
            pltpu.VMEM((2, HB, TAPS * EXC, LANES), bf16),
            pltpu.VMEM((BLK + 2 * HB, TAPS, EXC, LANES), f32),
            pltpu.VMEM(near_matrix.shape, bf16),
            pltpu.VMEM((n_pair, 2, QT, GRP, 256), bf16),
            pltpu.VMEM((n_dirs,) + weights.shape, bf16),
            pltpu.VMEM((n_space, MSG, LANES), bf16),
            pltpu.VMEM((n_space, MSG, LANES), bf16),
            pltpu.VMEM((2 * n_space, SPAN, LANES), f32),
            pltpu.VMEM((n_space, 2 * LIST, LANES), f32),
            pltpu.VMEM((n_space, 2 * ROWS, LANES), bf16),
            pltpu.VMEM((n_space, 2 * ROWS, LANES), bf16),
            pltpu.VMEM((2, 2, 16 + ROWS, 256), bf16),
            pltpu.VMEM((2, 2 * ROWS, GRP), f32),
            pltpu.SemaphoreType.DMA((2,)),
            pltpu.SemaphoreType.DMA((n_pair, 2)),
            pltpu.SemaphoreType.DMA,
            pltpu.SemaphoreType.DMA,
            pltpu.SemaphoreType.DMA((n_dirs,)),
            pltpu.SemaphoreType.DMA((n_dirs,)),
            pltpu.SemaphoreType.DMA((2,)),
            pltpu.SemaphoreType.DMA((2,)),
            pltpu.SemaphoreType.DMA,
            pltpu.SemaphoreType.DMA((n_space,)),
            pltpu.SemaphoreType.DMA((n_space,)),
            pltpu.SemaphoreType.DMA((n_space,)),
            pltpu.SemaphoreType.DMA((n_space,)),
        ],
        compiler_params=pltpu.CompilerParams(
            collective_id=0, has_side_effects=True, vmem_limit_bytes=56 * 1024 * 1024
        ),
        cost_estimate=pl.CostEstimate(
            flops=8 * QT * TAPS * EXC * cur * dirs // 2,
            bytes_accessed=2 * QT * cur * dirs,
            transcendentals=0,
        ),
    )(
        hq,
        blocks,
        radiation.reshape(QT, 2, GRP, dirs),
        near_matrix,
        weights,
        near_offset.reshape(-1),
        near_delay.reshape(-1),
        far_source.reshape(-1),
        far_delay.reshape(-1),
    )
    far_field = far.reshape(2, TAPS, HALF, cur).transpose(1, 0, 2, 3).reshape(TAPS, EXC, cur)
    return near, far_field


def solution(mesh):
    in_specs = (
        P(None, None, "space"),
        P(None, "space", None),
        P("space", None, None, None),
        P("space", None),
        P("space", None),
        P(),
        P(),
        P("space", None, "dirs"),
    )
    out_specs = (P("dirs", "space"), P(None, "dirs", "space"))
    part = functools.partial(local, mesh.shape["space"], mesh.shape["dirs"])
    return jax.shard_map(part, mesh=mesh, in_specs=in_specs, out_specs=out_specs, check_vma=False)
```

time: 302 us -> 113 us (0.37)
  local copies, waits for them, and re-layouts: 134 us -> 24.9 us
  Pallas kernels: 0 us -> 81.6 us
  blocking collectives: 70.3 us -> 0 us
  waiting for transfers between devices: 32.8 us -> 0 us
  other arithmetic: 22.5 us -> 4.99 us
  starting transfers between devices: 13.8 us -> 0 us
  between operations: 14.5 us -> 0.75 us
  matrix products: 12.4 us -> 0 us
    gather x9 -> x0, local copies, waits for them, and re-layouts: 94.4 us -> none  [the longest x8 92.4 us: translate(): jnp.take(flat_table, row_ids.reshape(-1), axis=0).reshape(table.shape)]
    pallas_call x0 -> x1, Pallas kernels: none -> 81.6 us  [local(): pl.pallas_call(functools.partial(kernel, n_space, n_dirs), out_shape=(jax...]
    all_gather x1 -> x0, blocking collectives: 37 us -> none  [local(): all_weights = lax.all_gather(far_weight, 'space', axis=0, tiled=True)]
    all_to_all x1 -> x0, blocking collectives: 33.3 us -> none  [local(): lax.all_to_all(translated, 'space', split_axis=0, concat_axis=2, tiled=True)]
    reduce_scatter x1 -> x0, waiting for transfers between devices: 28.6 us -> none  [local(): lax.psum_scatter(projected.reshape(lax.axis_size('dirs') * exc_part, tap_...]
    dot_general x8 -> x0, matrix products: 11.1 us -> none  [the longest x4 6.04 us: local(): jnp.einsum('gaek,gnk->eagn', delayed_in[:, first_row:first_row + tap_coun...]
    unnamed x85 -> x20, local copies, waits for them, and re-layouts: 11.8 us -> 2.82 us
    all_to_all x1 -> x0, starting transfers between devices: 8.79 us -> none  [local(): lax.all_to_all(ray_tiles, 'space', split_axis=2, concat_axis=0, tiled=True)]
  transfers between devices with their start and end apart: 4 -> 0, of which waited for: 2 -> 0; matrix products, arithmetic and copies ran while one was open for 7% -> 0% of each run, Pallas kernels for 0% -> 0%
where the time goes in v1:
time: 113 us; the launch traced here: 112 us
  Pallas kernels  81.6 us (72%)
  local copies, waits for them, and re-layouts  24.9 us (22%)
  other arithmetic  4.99 us (4%)
    pallas_call x1, Pallas kernels, local(): pl.pallas_call(functools.partial(kernel, n_space, n_dirs), out_shape=(jax...  81.6 us
    transpose x1, other arithmetic, local(): hq = stacked.transpose(1, 0, 2, 3).reshape(2, 2 * ROWS, QT * GRP)  4.99 us
    slice x4, local copies, waits for them, and re-layouts, local(): late[:, q:q + TAPS].reshape(2 * ROWS, 2, GRP)  4.57 us
    reshape x1, local copies, waits for them, and re-layouts, local(): hq = stacked.transpose(1, 0, 2, 3).reshape(2, 2 * ROWS, QT * GRP)  4.46 us
    another operation x4, local copies, waits for them, and re-layouts, local(): jnp.stack([late[:, q:q + TAPS].reshape(2 * ROWS, 2, GRP) for q in range(Q...  3.19 us
    transpose x1, local copies, waits for them, and re-layouts, local(): hq = stacked.transpose(1, 0, 2, 3).reshape(2, 2 * ROWS, QT * GRP)  2.92 us
    unnamed x20, local copies, waits for them, and re-layouts  2.82 us

profile of v1, /device:TPU:1, one launch (start us, length us, event | category | flops | bytes accessed | tf_op | source)
XLA Modules:
  0.0 112.3 jit_solution(18236476246430132249)
XLA Ops:
  0.6 0.0 copy-start
  0.6 1.6 %copy-done = bf16[32,32,1024]{2,1,0:T(8,128)(2,1)S(1)} copy-done((bf16[32,32,1024]{2,1,0:T(8,128)(2,1)S(1)}, bf16[32,32,1024]{2,1,0:T(8,128)(2,1)}, u32[]{:S(2)}) %copy-start) | copy-done | bytes 2097176
  2.3 0.3 copy.29
  2.6 1.3 %pad_slice_fusion.2 = (bf16[2,32,4,1024]{3,1,2,0:T(8,128)(2,1)S(1)}, bf16[2,32,4,1024]{3,1,2,0:T(8,128)(2,1)}, bf16[2,32,4,1024]{3,1,2,0:T(8,128)(2,1)}) fusion(bf16[2,32,4,1024]{3,1,2,0:T(8,128)(2,1)S(1)} %bitcast.17), kind=kLoop, calls=%fused_computation.3 | loop fusion | bytes 2097152 | tf_op jit(solution)/shard_map/slice | solution.py:376
  3.8 0.4 copy.19
  4.3 1.0 stack_reshape.13
  5.3 1.4 %copy.20 = bf16[2,32,4,1024]{3,2,1,0:T(4,128)(2,1)S(1)} copy(bf16[2,32,4,1024]{3,1,2,0:T(8,128)(2,1)} %get-tuple-element.7) | data formatting | bytes 1048576 | tf_op jit(solution)/shard_map/slice | solution.py:376
  6.7 1.0 stack_reshape.14
  7.7 1.4 %copy.21 = bf16[2,32,4,1024]{3,2,1,0:T(4,128)(2,1)S(1)} copy(bf16[2,32,4,1024]{3,1,2,0:T(8,128)(2,1)} %get-tuple-element.8) | data formatting | bytes 1048576 | tf_op jit(solution)/shard_map/slice | solution.py:376
  9.2 1.0 stack_reshape.15
  10.1 0.4 copy.18
  10.6 0.2 stack_reshape.12
  10.8 5.0 %maximum_bitcast_fusion = bf16[2,256,4,512]{3,0,1,2:T(2,128)(2,1)S(1)} fusion(bf16[256,2,1,512]{3,1,0,2:T(2,128)(2,1)} %stack_reshape.15, bf16[256,2,1,512]{3,1,0,2:T(2,128)(2,1)} %stack_reshape.14, bf16[256,2,1,512]{3,1,0,2:T(2,128)(2,1)} %stack_reshape.13, bf16[256,2,1,512]{3,1,0,2:T(2,128)(2,1)S(1)} %stack_reshape.12), kind=kLoop, calls=%fused_computation | loop fusion | flops 3145728 | bytes 4194304 | tf_op jit(solution)/shard_map/transpose | solution.py:378
  15.8 2.9 %copy.22 = bf16[2,256,4,512]{3,2,1,0:T(4,128)(2,1)} copy(bf16[2,256,4,512]{3,0,1,2:T(2,128)(2,1)S(1)} %maximum_bitcast_fusion) | data formatting | bytes 4194304 | tf_op jit(solution)/shard_map/transpose | solution.py:378
  18.7 4.5 %reshape.38.hq_ref = bf16[2,256,2048]{2,1,0:T(8,128)(2,1)} reshape(bf16[2,256,4,512]{3,2,1,0:T(4,128)(2,1)} %copy.22) | data formatting | bytes 4194304 | tf_op jit(solution)/shard_map/reshape | solution.py:378
  23.1 0.0 copy-start.3
  23.1 0.0 copy-start.4
  23.1 0.0 copy-start.1
  23.1 0.0 copy-start.5
  23.2 0.0 copy-start.6
  23.2 0.1 copy.30
  23.3 0.9 copy.33
  24.2 0.0 copy-done.3
  24.2 0.1 copy.26
  24.3 0.7 reshape.44.src_ref
  25.0 0.0 copy-done.4
  25.0 0.1 copy.27
  25.1 0.7 reshape.45.lag_ref
  25.7 0.0 copy-done.1
  25.8 0.6 copy.34
  26.4 0.0 copy-done.5
  26.4 0.6 reshape.42.off_ref
  27.0 0.0 copy-done.6
  27.0 0.6 reshape.43.del_ref
  27.6 81.6 %shard_map.95 = (bf16[256,1024]{1,0:T(8,128)(2,1)}, bf16[8,1024]{1,0:T(8,128)(2,1)}) custom-call(bf16[2,256,2048]{2,1,0:T(8,128)(2,1)} %reshape.38.hq_ref, bf16[8,256,128]{2,1,0:T(8,128)(2,1)} %bitcast.21, bf16[4,2,512,2048]{3,2,1,0:T(8,128)(2,1)} %bitcast.23, bf16[8,8,128,128]{3,2,1,0:T(8,128)(2,1)} %mat_ref.1, bf16[4,16,128]{2,1,0:T(8,128)(2,1)} %bitcast.22, ...), custom_call_target="tpu_custom_call" | custom-call | flops 8589934592 | bytes 16777216 | tf_op jit(solution)/shard_map/pallas_call | solution.py:385
  109.2 0.0 copy-start.2
  109.2 1.2 %reshape.46 = bf16[2,32,4,1024]{3,2,1,0:T(4,128)(2,1)S(1)} reshape(bf16[256,1024]{1,0:T(8,128)(2,1)} %get-tuple-element.5) | data formatting | bytes 1048576 | tf_op jit(solution)/shard_map/reshape | solution.py:442
  110.5 0.3 copy.28
  110.8 0.9 reshape.47
  111.7 0.0 copy-done.2
  111.7 0.6 copy.36
  (3 shorter events, 0.1 us)
Async XLA Ops:
  0.6 1.6 %copy-start = (bf16[32,32,1024]{2,1,0:T(8,128)(2,1)S(1)}, bf16[32,32,1024]{2,1,0:T(8,128)(2,1)}, u32[]{:S(2)}) copy-start(bf16[32,32,1024]{2,1,0:T(8,128)(2,1)} %param.8) | copy-start | bytes 6291460
  23.1 1.1 copy-start.3
  23.1 1.8 %copy-start.4 = (s32[64,8]{0,1:T(8,128)S(1)}, s32[64,8]{0,1:T(8,128)}, u32[]{:S(2)}) copy-start(s32[64,8]{0,1:T(8,128)} %param.14) | copy-start | bytes 6148
  23.1 2.6 %copy-start.1 = (bf16[2,8,512]{2,1,0:T(8,128)(2,1)S(1)}, bf16[2,8,512]{2,1,0:T(8,128)(2,1)}, u32[]{:S(2)}) copy-start(bf16[2,8,512]{2,1,0:T(8,128)(2,1)} %param.15) | copy-start | bytes 49156
  23.1 3.2 %copy-start.5 = (s32[8,8]{1,0:T(8,128)S(1)}, s32[8,8]{1,0:T(8,128)}, u32[]{:S(2)}) copy-start(s32[8,8]{1,0:T(8,128)} %param.11) | copy-start | bytes 772
  23.2 3.9 %copy-start.6 = (s32[8,8]{1,0:T(8,128)S(1)}, s32[8,8]{1,0:T(8,128)}, u32[]{:S(2)}) copy-start(s32[8,8]{1,0:T(8,128)} %param.12) | copy-start | bytes 772
  109.2 2.5 %copy-start.2 = (bf16[8,1024]{1,0:T(8,128)(2,1)S(1)}, bf16[8,1024]{1,0:T(8,128)(2,1)}, u32[]{:S(2)}) copy-start(bf16[8,1024]{1,0:T(8,128)(2,1)} %get-tuple-element.11) | copy-start | bytes 49156

commit v2 on v1

--- a/solution.py
+++ b/solution.py
@@ -26,8 +26,7 @@
 def kernel(
     n_space,
     n_dirs,
-    hq_ref,
-    hb_ref,
+    hist_ref,
     rad_ref,
     mat_ref,
     w_ref,
@@ -37,6 +36,7 @@
     lag_ref,
     far_ref,
     near_ref,
+    hist,
     hq,
     hb,
     halo,
@@ -52,7 +52,7 @@
     recv2,
     padded,
     acc,
-    hq_sem,
+    hist_sem,
     rad_sem,
     mat_sem,
     w_sem,
@@ -67,7 +67,7 @@
     recv2_sem,
 ):
     n_pair = n_space // 4
-    per_plane = w_ref.shape[0]
+    per_plane = w_ref.shape[1] // LANES
     me = lax.axis_index("space")
     plane = lax.axis_index("dirs")
     my_pair = lax.div(me, 4)
@@ -133,11 +133,19 @@
             device_id_type=MESH,
         )
 
-    hq_copy = pltpu.make_async_copy(hq_ref, hq, hq_sem.at[0])
-    hb_copy = pltpu.make_async_copy(hb_ref, hb, hq_sem.at[1])
+    rows_at = pl.ds(pl.multiple_of(lax.div(plane, 2) * 16, 16), 16)
+    hist_copy = pltpu.make_async_copy(hist_ref.at[:, rows_at, :], hist, hist_sem)
     mat_copy = pltpu.make_async_copy(mat_ref, mat, mat_sem)
-    w_copy = pltpu.make_async_copy(w_ref, wz.at[plane], w_sem)
-
+    w_copies = [
+        pltpu.make_async_copy(
+            w_ref.at[:, pl.ds(j * LANES, LANES)], wz.at[plane, j], w_sem.at[j]
+        )
+        for j in range(per_plane)
+    ]
+
+    hist_copy.start()
+    for copy in w_copies:
+        copy.start()
     barrier = pltpu.get_barrier_semaphore()
 
     def greet(i, carry):
@@ -152,22 +160,54 @@
             barrier, inc=1, device_id={"dirs": lax.rem(plane + i, n_dirs)}, device_id_type=MESH
         )
 
-    w_copy.start()
-    hq_copy.start()
-
     def fetch(i, carry):
         for g in range(2):
             rad_copy(pair_at(i), g).start()
         return carry
 
     lax.fori_loop(0, n_pair, fetch, 0)
-    hb_copy.start()
     mat_copy.start()
-    w_copy.wait()
+
+    hist_copy.wait()
+    low_half = lax.rem(plane, 2) == 0
+
+    def spread(i, carry):
+        pair = []
+        for a in range(2):
+            rows = hist[2 * i + a].astype(jnp.float32)
+            rows = jnp.where(low_half, rows[0:EXC], rows[EXC : 2 * EXC])
+            for b in range(BLK):
+                ext[HB + b, 2 * i + a] = rows[:, b * LANES : (b + 1) * LANES]
+            pair.append(rows)
+        rows = jnp.concatenate(pair, axis=0).astype(jnp.bfloat16)
+        for b in range(BLK):
+            hb[b, pl.ds(pl.multiple_of(i * 16, 16), 16), :] = rows[:, b * LANES : (b + 1) * LANES]
+        return carry
+
+    lax.fori_loop(0, TAPS // 2, spread, 0)
+    ext[HB : HB + BLK, TAPS : TAPS + QT] = jnp.zeros((BLK, QT, EXC, LANES), jnp.float32)
+
+    def stack(i, carry):
+        for g in range(2):
+            for blk in range(BLK // 2):
+                for q in range(QT):
+                    taps = [ext[HB + g * (BLK // 2) + blk, 4 * i + q + a] for a in range(4)]
+                    cols = q * GRP + blk * LANES
+                    for c in range(2):
+                        rows = [tap[c * HALF : (c + 1) * HALF] for tap in taps]
+                        hq[
+                            g,
+                            pl.ds(pl.multiple_of(c * ROWS + i * 16, 16), 16),
+                            cols : cols + LANES,
+                        ] = jnp.concatenate(rows, axis=0).astype(jnp.bfloat16)
+        return carry
+
+    lax.fori_loop(0, TAPS // 4, stack, 0)
+    for copy in w_copies:
+        copy.wait()
     pl.semaphore_wait(barrier, n_space - 1 + n_dirs - 1)
     for i in range(1, n_dirs):
         z_copy(lax.rem(plane + i, n_dirs)).start()
-    hq_copy.wait()
 
     def aggregate(p):
         for g in range(2):
@@ -212,19 +252,12 @@
 
     lax.fori_loop(1, n_pair, agg_step, 0)
 
-    hb_copy.wait()
     halo_copy(0).start()
     halo_copy(1).start()
 
     table[:, ROWS:SPAN, :] = jnp.zeros((table.shape[0], SPAN - ROWS, LANES), jnp.float32)
     acc[...] = jnp.zeros_like(acc)
     padded[:, :, 0:16, :] = jnp.zeros((2, 2, 16, 256), jnp.bfloat16)
-
-    def own_blocks(b, carry):
-        ext[HB + b] = hb[b].astype(jnp.float32).reshape(TAPS, EXC, LANES)
-        return carry
-
-    lax.fori_loop(0, BLK, own_blocks, 0)
 
     def take_in(i, carry):
         p = pair_from(i)
@@ -256,11 +289,10 @@
                 weights = wtab[t, g * LIST : (g + 1) * LIST, :]
                 total = jnp.zeros((ROWS, LANES), jnp.float32)
                 for slot in range(LIST):
-                    entry = (2 * t + g) * LIST + slot
-                    first = lag_ref[entry] * HALF
+                    first = lag_ref[slot, 2 * t + g] * HALF
                     total = (
                         total
-                        + weights[slot : slot + 1, :] * table[src_ref[entry], pl.ds(first, ROWS), :]
+                        + weights[slot : slot + 1, :] * table[src_ref[slot, 2 * t + g], pl.ds(first, ROWS), :]
                     )
                 send2[t, g * ROWS : (g + 1) * ROWS, :] = total.astype(jnp.bfloat16)
 
@@ -280,8 +312,8 @@
         halo_copy(side).wait_recv()
 
     def halo_blocks(b, carry):
-        ext[b] = halo[0, b].astype(jnp.float32).reshape(TAPS, EXC, LANES)
-        ext[HB + BLK + b] = halo[1, b].astype(jnp.float32).reshape(TAPS, EXC, LANES)
+        ext[b, 0:TAPS] = halo[0, b].astype(jnp.float32).reshape(TAPS, EXC, LANES)
+        ext[HB + BLK + b, 0:TAPS] = halo[1, b].astype(jnp.float32).reshape(TAPS, EXC, LANES)
         return carry
 
     lax.fori_loop(0, HB, halo_blocks, 0)
@@ -290,10 +322,10 @@
     for b in range(BLK):
         near = jnp.zeros((EXC, LANES), jnp.float32)
         for slot in range(NEAR):
-            shift = off_ref[b * NEAR + slot]
+            shift = off_ref[b, slot]
             block = me * BLK + b + shift
             inside = jnp.logical_and(block >= 0, block < n_space * BLK)
-            values = ext[b + HB + shift, del_ref[b * NEAR + slot]]
+            values = ext[b + HB + shift, del_ref[b, slot]]
             values = jnp.where(inside, values, 0.0).astype(jnp.bfloat16)
             near = near + lax.dot_general(
                 values,
@@ -338,8 +370,20 @@
         return carry
 
     lax.fori_loop(0, n_pair, project, 0)
-    for g in range(2):
-        far_ref[:, g * GRP : (g + 1) * GRP] = acc[g].astype(jnp.bfloat16)
+
+    def finish(a, carry):
+        for g in range(2):
+            halves = [
+                acc[g, pl.ds(c * ROWS + a * 2 * HALF, 2 * HALF), :] for c in range(2)
+            ]
+            for i in range(2):
+                rows = [half[i * HALF : (i + 1) * HALF] for half in halves]
+                far_ref[2 * a + i, :, g * GRP : (g + 1) * GRP] = jnp.concatenate(
+                    rows, axis=0
+                ).astype(jnp.bfloat16)
+        return carry
+
+    lax.fori_loop(0, TAPS // 2, finish, 0)
 
     def drain(i, carry):
         t = lax.rem(me + i, n_space)
@@ -368,15 +412,7 @@
 ):
     cur = history.shape[2]
     dirs = radiation.shape[2]
-    own = lax.dynamic_slice_in_dim(history, lax.axis_index("dirs") * EXC, EXC, 1)
-    blocks = own.reshape(TAPS * EXC, BLK, LANES).transpose(1, 0, 2)
-    rows = own.reshape(TAPS, 2, HALF, cur).transpose(1, 0, 2, 3)
-    late = jnp.concatenate([rows, jnp.zeros((2, QT - 1, HALF, cur), rows.dtype)], axis=1)
-    stacked = jnp.stack(
-        [late[:, q : q + TAPS].reshape(2 * ROWS, 2, GRP) for q in range(QT)], axis=2
-    )
-    hq = stacked.transpose(1, 0, 2, 3).reshape(2, 2 * ROWS, QT * GRP)
-    weights = far_weight.reshape(2 * LIST, -1, LANES).transpose(1, 0, 2)
+    weights = far_weight.reshape(2 * LIST, -1)
     n_pair = n_space // 4
     any_spec = pl.BlockSpec(memory_space=pl.ANY)
     smem = pl.BlockSpec(memory_space=pltpu.SMEM)
@@ -385,19 +421,20 @@
     far, near = pl.pallas_call(
         functools.partial(kernel, n_space, n_dirs),
         out_shape=(
-            jax.ShapeDtypeStruct((2 * ROWS, cur), bf16),
+            jax.ShapeDtypeStruct((TAPS, EXC, cur), bf16),
             jax.ShapeDtypeStruct((EXC, cur), bf16),
         ),
-        in_specs=[any_spec] * 5 + [smem] * 4,
+        in_specs=[any_spec] * 4 + [smem] * 4,
         out_specs=(vmem, vmem),
         scratch_shapes=[
+            pltpu.VMEM((TAPS, 2 * EXC, cur), bf16),
             pltpu.VMEM((2, 2 * ROWS, QT * GRP), bf16),
             pltpu.VMEM((BLK, TAPS * EXC, LANES), bf16),
             pltpu.VMEM((2, HB, TAPS * EXC, LANES), bf16),
-            pltpu.VMEM((BLK + 2 * HB, TAPS, EXC, LANES), f32),
+            pltpu.VMEM((BLK + 2 * HB, TAPS + QT, EXC, LANES), f32),
             pltpu.VMEM(near_matrix.shape, bf16),
             pltpu.VMEM((n_pair, 2, QT, GRP, 256), bf16),
-            pltpu.VMEM((n_dirs,) + weights.shape, bf16),
+            pltpu.VMEM((n_dirs, weights.shape[1] // LANES, 2 * LIST, LANES), bf16),
             pltpu.VMEM((n_space, MSG, LANES), bf16),
             pltpu.VMEM((n_space, MSG, LANES), bf16),
             pltpu.VMEM((2 * n_space, SPAN, LANES), f32),
@@ -406,10 +443,10 @@
             pltpu.VMEM((n_space, 2 * ROWS, LANES), bf16),
             pltpu.VMEM((2, 2, 16 + ROWS, 256), bf16),
             pltpu.VMEM((2, 2 * ROWS, GRP), f32),
-            pltpu.SemaphoreType.DMA((2,)),
+            pltpu.SemaphoreType.DMA,
             pltpu.SemaphoreType.DMA((n_pair, 2)),
             pltpu.SemaphoreType.DMA,
-            pltpu.SemaphoreType.DMA,
+            pltpu.SemaphoreType.DMA((weights.shape[1] // LANES,)),
             pltpu.SemaphoreType.DMA((n_dirs,)),
             pltpu.SemaphoreType.DMA((n_dirs,)),
             pltpu.SemaphoreType.DMA((2,)),
@@ -429,18 +466,16 @@
             transcendentals=0,
         ),
     )(
-        hq,
-        blocks,
+        history,
         radiation.reshape(QT, 2, GRP, dirs),
         near_matrix,
         weights,
-        near_offset.reshape(-1),
-        near_delay.reshape(-1),
-        far_source.reshape(-1),
-        far_delay.reshape(-1),
+        near_offset,
+        near_delay,
+        far_source.T,
+        far_delay.T,
     )
-    far_field = far.reshape(2, TAPS, HALF, cur).transpose(1, 0, 2, 3).reshape(TAPS, EXC, cur)
-    return near, far_field
+    return near, far
 
 
 def solution(mesh):

time: 113 us -> 86.1 us (0.76)
  local copies, waits for them, and re-layouts: 24.9 us -> 3.19 us
  other arithmetic: 4.99 us -> 0 us
    reshape x10 -> x0, local copies, waits for them, and re-layouts: 10.7 us -> none  [the longest x1 4.46 us: local(): hq = stacked.transpose(1, 0, 2, 3).reshape(2, 2 * ROWS, QT * GRP)]
    transpose x1 -> x0, other arithmetic: 4.99 us -> none  [local(): hq = stacked.transpose(1, 0, 2, 3).reshape(2, 2 * ROWS, QT * GRP)]
    slice x4 -> x0, local copies, waits for them, and re-layouts: 4.57 us -> none  [local(): late[:, q:q + TAPS].reshape(2 * ROWS, 2, GRP)]
    transpose x3 -> x0, local copies, waits for them, and re-layouts: 3.6 us -> none  [the longest x1 2.92 us: local(): hq = stacked.transpose(1, 0, 2, 3).reshape(2, 2 * ROWS, QT * GRP)]
    another operation x4 -> x0, local copies, waits for them, and re-layouts: 3.19 us -> none  [local(): jnp.stack([late[:, q:q + TAPS].reshape(2 * ROWS, 2, GRP) for q in range(Q...]
    unnamed x20 -> x2, local copies, waits for them, and re-layouts: 2.82 us -> 3.19 us
where the time goes in v2:
time: 86.1 us; the launch traced here: 85.8 us
  Pallas kernels  82 us (95%)
  local copies, waits for them, and re-layouts  3.19 us (4%)
    pallas_call x1, Pallas kernels, local(): pl.pallas_call(functools.partial(kernel, n_space, n_dirs), out_shape=(jax...  82 us
    unnamed x2, local copies, waits for them, and re-layouts  3.19 us

profile of v2, /device:TPU:1, one launch (start us, length us, event | category | flops | bytes accessed | tf_op | source)
XLA Modules:
  0.0 85.8 jit_solution(17375058657804815217)
XLA Ops:
  0.6 82.0 %shard_map.95 = (bf16[32,8,1024]{2,1,0:T(8,128)(2,1)}, bf16[8,1024]{1,0:T(8,128)(2,1)}) custom-call(bf16[32,32,1024]{2,1,0:T(8,128)(2,1)} %hist_ref.1, bf16[4,2,512,2048]{3,2,1,0:T(8,128)(2,1)} %bitcast.4, bf16[8,8,128,128]{3,2,1,0:T(8,128)(2,1)} %mat_ref.1, bf16[16,512]{1,0:T(8,128)(2,1)} %bitcast.5, s32[8,8]{1,0:T(8,128)} %off_ref.1, s32[8,8]{1,0:T(8,128)} %del_ref.1, ...), custom_call_target="tpu_custom_call" | custom-call | flops 8589934592 | bytes 16777216 | tf_op jit(solution)/shard_map/pallas_call | solution.py:421
  82.6 1.3 %copy.12 = bf16[8,1024]{1,0:T(8,128)(2,1)} copy(bf16[8,1024]{1,0:T(8,128)(2,1)} %get-tuple-element.8) | data formatting | bytes 32768
  84.0 1.9 %copy.13 = bf16[32,8,1024]{2,1,0:T(8,128)(2,1)} copy(bf16[32,8,1024]{2,1,0:T(8,128)(2,1)} %get-tuple-element.9) | data formatting | bytes 1048576

commit v3 on v2

--- a/solution.py
+++ b/solution.py
@@ -21,6 +21,9 @@
 SPAN = ROWS + 16 * HALF
 GRP = 512
 MSG = 2 * ROWS + 2 * LIST
+SIDE = 4
+TIES = ((2, 2), (1, 2), (3, 2), (0, 2), (2, 3), (2, 0), (2, 1))
+N_RELAY = 4 * len(TIES)
 
 
 def kernel(
@@ -50,6 +53,8 @@
     wtab,
     send2,
     recv2,
+    relay1,
+    relay2,
     padded,
     acc,
     hist_sem,
@@ -65,19 +70,144 @@
     recv1_sem,
     send2_sem,
     recv2_sem,
+    relay1_sem,
+    relay2_sem,
+    forward1_sem,
+    forward2_sem,
 ):
     n_pair = n_space // 4
     per_plane = w_ref.shape[1] // LANES
     me = lax.axis_index("space")
     plane = lax.axis_index("dirs")
-    my_pair = lax.div(me, 4)
+    my_core = lax.rem(me, 2)
+    my_x = lax.rem(lax.div(me, 2), SIDE)
+    my_y = lax.div(me, 2 * SIDE)
     right, left = lax.rem(me + 1, n_space), lax.rem(me + n_space - 1, n_space)
 
+    def device(x, y, c):
+        return (lax.rem(y, SIDE) * SIDE + lax.rem(x, SIDE)) * 2 + c
+
     def pair_at(i):
-        return lax.rem(my_pair + i, n_pair)
+        y = lax.rem(my_y + 2 + lax.div(i, 2), SIDE)
+        half = lax.rem(lax.div(my_x, 2) + 1 + i, 2)
+        return 2 * y + half
 
     def pair_from(i):
-        return lax.rem(my_pair + n_pair - i, n_pair)
+        y = lax.rem(my_y + SIDE - 1 + lax.div(i, 2), SIDE)
+        half = lax.rem(lax.div(my_x, 2) + i, 2)
+        return 2 * y + half
+
+    def steps_to(t):
+        dx = lax.rem(lax.rem(lax.div(t, 2), SIDE) + SIDE - my_x, SIDE)
+        dy = lax.rem(lax.div(t, 2 * SIDE) + SIDE - my_y, SIDE)
+        return dx, dy, jnp.logical_or(dx == 2, dy == 2)
+
+    def half_rows(h, rows):
+        return pl.ds(0, ROWS) if h == 0 else pl.ds(ROWS, rows - ROWS)
+
+    def remote(src, dst, send, recv, t):
+        return pltpu.make_async_remote_copy(
+            src_ref=src,
+            dst_ref=dst,
+            send_sem=send,
+            recv_sem=recv,
+            device_id={"space": t},
+            device_id_type=MESH,
+        )
+
+    exchanges = (
+        (MSG, send1, recv1, relay1, send1_sem, recv1_sem, relay1_sem, forward1_sem),
+        (2 * ROWS, send2, recv2, relay2, send2_sem, recv2_sem, relay2_sem, forward2_sem),
+    )
+
+    def whole(ex, t, slot):
+        rows, send, recv, _, send_sem, recv_sem, _, _ = exchanges[ex]
+        return remote(send.at[t], recv.at[slot], send_sem.at[t, 0], recv_sem.at[slot, 0], t)
+
+    def half(ex, t, slot, h):
+        rows, send, recv, _, send_sem, recv_sem, _, _ = exchanges[ex]
+        at = half_rows(h, rows)
+        return remote(
+            send.at[t, at], recv.at[slot, at], send_sem.at[t, h], recv_sem.at[slot, h], t
+        )
+
+    def post(ex, t):
+        rows, send, recv, relay, send_sem, recv_sem, relay_sem, _ = exchanges[ex]
+        dx, dy, tie = steps_to(t)
+
+        @pl.when(t == me)
+        def _():
+            pltpu.make_async_copy(send.at[t], recv.at[t], own_sem).start()
+
+        @pl.when(jnp.logical_and(t != me, jnp.logical_not(tie)))
+        def _():
+            whole(ex, t, me).start()
+
+        @pl.when(tie)
+        def _():
+            along_x = jnp.where(dx == 2, 1, 0)
+            along_y = jnp.where(dy == 2, 1, 0)
+            first = jnp.where(dx == 0, 3, jnp.where(dx == 1, 1, jnp.where(dx == 3, 2, 0)))
+            kind = jnp.where(dy == 2, first, 4 + lax.rem(dy + 1, SIDE))
+            for h in range(2):
+                turn = 1 if h == 0 else SIDE - 1
+                by = device(my_x + turn * along_x, my_y + turn * along_y, lax.rem(t, 2))
+                slot = kind * 4 + 2 * h + my_core
+                at = half_rows(h, rows)
+                remote(
+                    send.at[t, at],
+                    relay.at[slot, pl.ds(0, at.size)],
+                    send_sem.at[t, h],
+                    relay_sem.at[slot],
+                    by,
+                ).start()
+
+    def pass_on(ex, slot, start):
+        rows, send, recv, relay, _, recv_sem, relay_sem, forward_sem = exchanges[ex]
+        (dx, dy), h, c = TIES[slot // 4], slot // 2 % 2, slot % 2
+        back = SIDE - 1 if h == 0 else 1
+        x = my_x + back * (dx == 2)
+        y = my_y + back * (dy == 2)
+        sender, target = device(x, y, c), device(x + dx, y + dy, my_core)
+        at = half_rows(h, rows)
+        held = relay.at[slot, pl.ds(0, at.size)]
+        onward = remote(
+            held, recv.at[sender, at], forward_sem.at[slot], recv_sem.at[sender, h], target
+        )
+        if start:
+            remote(held, held, forward_sem.at[slot], relay_sem.at[slot], target).wait_recv()
+            onward.start()
+        else:
+            onward.wait_send()
+
+    def arrival(ex, s):
+        rows, send, recv, _, _, _, _, _ = exchanges[ex]
+        tie = steps_to(s)[2]
+
+        @pl.when(s == me)
+        def _():
+            pltpu.make_async_copy(send.at[s], recv.at[s], own_sem).wait()
+
+        @pl.when(jnp.logical_and(s != me, jnp.logical_not(tie)))
+        def _():
+            whole(ex, s, s).wait_recv()
+
+        @pl.when(tie)
+        def _():
+            for h in range(2):
+                half(ex, s, s, h).wait_recv()
+
+    def sent(ex, t):
+        tie = steps_to(t)[2]
+
+        @pl.when(jnp.logical_not(tie))
+        def _():
+            whole(ex, t, me).wait_send()
+
+        @pl.when(tie)
+        def _():
+            for h in range(2):
+                half(ex, t, me, h).wait_send()
 
     def rad_copy(p, g):
         cols = pl.ds(pl.multiple_of(p * 256, 256), 256)
@@ -100,26 +230,6 @@
             send_sem=z_send.at[frm],
             recv_sem=z_recv.at[frm],
             device_id={"dirs": frm},
-            device_id_type=MESH,
-        )
-
-    def to_translator(t, slot):
-        return pltpu.make_async_remote_copy(
-            src_ref=send1.at[t],
-            dst_ref=recv1.at[slot],
-            send_sem=send1_sem.at[t],
-            recv_sem=recv1_sem.at[slot],
-            device_id={"space": t},
-            device_id_type=MESH,
-        )
-
-    def to_owner(t, slot):
-        return pltpu.make_async_remote_copy(
-            src_ref=send2.at[t],
-            dst_ref=recv2.at[slot],
-            send_sem=send2_sem.at[t],
-            recv_sem=recv2_sem.at[slot],
-            device_id={"space": t},
             device_id_type=MESH,
         )
 
@@ -186,6 +296,14 @@
 
     lax.fori_loop(0, TAPS // 2, spread, 0)
     ext[HB : HB + BLK, TAPS : TAPS + QT] = jnp.zeros((BLK, QT, EXC, LANES), jnp.float32)
+
+    for copy in w_copies:
+        copy.wait()
+    pl.semaphore_wait(barrier, n_space - 1 + n_dirs - 1)
+    for i in range(1, n_dirs):
+        z_copy(lax.rem(plane + i, n_dirs)).start()
+    halo_copy(0).start()
+    halo_copy(1).start()
 
     def stack(i, carry):
         for g in range(2):
@@ -203,12 +321,6 @@
         return carry
 
     lax.fori_loop(0, TAPS // 4, stack, 0)
-    for copy in w_copies:
-        copy.wait()
-    pl.semaphore_wait(barrier, n_space - 1 + n_dirs - 1)
-    for i in range(1, n_dirs):
-        z_copy(lax.rem(plane + i, n_dirs)).start()
-
     def aggregate(p):
         for g in range(2):
             rad_copy(p, g).wait()
@@ -230,19 +342,12 @@
             for c in range(2):
                 t = 4 * p + 2 * jj + c
                 send1[t, pl.ds(2 * ROWS, 2 * LIST), :] = weights
-
-                @pl.when(t != me)
-                def _():
-                    to_translator(t, me).start()
-
-                @pl.when(t == me)
-                def _():
-                    pltpu.make_async_copy(send1.at[t], recv1.at[t], own_sem).start()
-
-    aggregate(my_pair)
+                post(0, t)
+
+    aggregate(pair_at(0))
     for i in range(1, n_dirs):
         z_arrival(lax.rem(plane + n_dirs - i, n_dirs)).wait_recv()
-    dispatch(my_pair)
+    dispatch(pair_at(0))
 
     def agg_step(i, carry):
         p = pair_at(i)
@@ -252,8 +357,8 @@
 
     lax.fori_loop(1, n_pair, agg_step, 0)
 
-    halo_copy(0).start()
-    halo_copy(1).start()
+    for slot in range(N_RELAY):
+        pass_on(0, slot, True)
 
     table[:, ROWS:SPAN, :] = jnp.zeros((table.shape[0], SPAN - ROWS, LANES), jnp.float32)
     acc[...] = jnp.zeros_like(acc)
@@ -264,14 +369,7 @@
         for j in range(4):
             s = 4 * p + j
 
-            @pl.when(s != me)
-            def _():
-                to_translator(s, s).wait_recv()
-
-            @pl.when(s == me)
-            def _():
-                pltpu.make_async_copy(send1.at[s], recv1.at[s], own_sem).wait()
-
+            arrival(0, s)
             for g in range(2):
                 table[2 * s + g, 0:ROWS, :] = recv1[s, g * ROWS : (g + 1) * ROWS, :].astype(
                     jnp.float32
@@ -295,18 +393,12 @@
                         + weights[slot : slot + 1, :] * table[src_ref[slot, 2 * t + g], pl.ds(first, ROWS), :]
                     )
                 send2[t, g * ROWS : (g + 1) * ROWS, :] = total.astype(jnp.bfloat16)
-
-            @pl.when(t != me)
-            def _():
-                to_owner(t, me).start()
-
-            @pl.when(t == me)
-            def _():
-                pltpu.make_async_copy(send2.at[t], recv2.at[t], own_sem).start()
-
+            post(1, t)
         return carry
 
     lax.fori_loop(0, n_pair, translate, 0)
+    for slot in range(N_RELAY):
+        pass_on(1, slot, True)
 
     for side in range(2):
         halo_copy(side).wait_recv()
@@ -339,15 +431,7 @@
         p = pair_from(i)
         for j in range(4):
             s = 4 * p + j
-
-            @pl.when(s != me)
-            def _():
-                to_owner(s, s).wait_recv()
-
-            @pl.when(s == me)
-            def _():
-                pltpu.make_async_copy(send2.at[s], recv2.at[s], own_sem).wait()
-
+            arrival(1, s)
             jj, c = j // 2, j % 2
             for g in range(2):
                 padded[g, c, 16 : 16 + ROWS, jj * LANES : (jj + 1) * LANES] = recv2[
@@ -387,11 +471,14 @@
 
     def drain(i, carry):
         t = lax.rem(me + i, n_space)
-        to_translator(t, me).wait_send()
-        to_owner(t, me).wait_send()
+        sent(0, t)
+        sent(1, t)
         return carry
 
     lax.fori_loop(1, n_space, drain, 0)
+    for slot in range(N_RELAY):
+        pass_on(0, slot, False)
+        pass_on(1, slot, False)
     for i in range(1, n_dirs):
         z_copy(lax.rem(plane + i, n_dirs)).wait_send()
     for side in range(2):
@@ -441,6 +528,8 @@
             pltpu.VMEM((n_space, 2 * LIST, LANES), f32),
             pltpu.VMEM((n_space, 2 * ROWS, LANES), bf16),
             pltpu.VMEM((n_space, 2 * ROWS, LANES), bf16),
+            pltpu.VMEM((N_RELAY, MSG - ROWS, LANES), bf16),
+            pltpu.VMEM((N_RELAY, ROWS, LANES), bf16),
             pltpu.VMEM((2, 2, 16 + ROWS, 256), bf16),
             pltpu.VMEM((2, 2 * ROWS, GRP), f32),
             pltpu.SemaphoreType.DMA,
@@ -452,10 +541,14 @@
             pltpu.SemaphoreType.DMA((2,)),
             pltpu.SemaphoreType.DMA((2,)),
             pltpu.SemaphoreType.DMA,
-            pltpu.SemaphoreType.DMA((n_space,)),
-            pltpu.SemaphoreType.DMA((n_space,)),
-            pltpu.SemaphoreType.DMA((n_space,)),
-            pltpu.SemaphoreType.DMA((n_space,)),
+            pltpu.SemaphoreType.DMA((n_space, 2)),
+            pltpu.SemaphoreType.DMA((n_space, 2)),
+            pltpu.SemaphoreType.DMA((n_space, 2)),
+            pltpu.SemaphoreType.DMA((n_space, 2)),
+            pltpu.SemaphoreType.DMA((N_RELAY,)),
+            pltpu.SemaphoreType.DMA((N_RELAY,)),
+            pltpu.SemaphoreType.DMA((N_RELAY,)),
+            pltpu.SemaphoreType.DMA((N_RELAY,)),
         ],
         compiler_params=pltpu.CompilerParams(
             collective_id=0, has_side_effects=True, vmem_limit_bytes=56 * 1024 * 1024

time: 86.1 us -> 87.1 us (1.012)
  the two profiles are of different devices: /device:TPU:1 before, /device:TPU:2 now
where the time goes in v3:
time: 87.1 us; the launch traced here: 86.8 us
  Pallas kernels  83 us (95%)
  local copies, waits for them, and re-layouts  3.19 us (4%)
    pallas_call x1, Pallas kernels, local(): pl.pallas_call(functools.partial(kernel, n_space, n_dirs), out_shape=(jax...  83 us
    unnamed x2, local copies, waits for them, and re-layouts  3.19 us

profile of v3, /device:TPU:2, one launch (start us, length us, event | category | flops | bytes accessed | tf_op | source)
XLA Modules:
  0.0 86.8 jit_solution(16498492434000943148)
XLA Ops:
  0.6 83.0 %shard_map.95 = (bf16[32,8,1024]{2,1,0:T(8,128)(2,1)}, bf16[8,1024]{1,0:T(8,128)(2,1)}) custom-call(bf16[32,32,1024]{2,1,0:T(8,128)(2,1)} %hist_ref.1, bf16[4,2,512,2048]{3,2,1,0:T(8,128)(2,1)} %bitcast.4, bf16[8,8,128,128]{3,2,1,0:T(8,128)(2,1)} %mat_ref.1, bf16[16,512]{1,0:T(8,128)(2,1)} %bitcast.5, s32[8,8]{1,0:T(8,128)} %off_ref.1, s32[8,8]{1,0:T(8,128)} %del_ref.1, ...), custom_call_target="tpu_custom_call" | custom-call | flops 8589934592 | bytes 16777216 | tf_op jit(solution)/shard_map/pallas_call | solution.py:508
  83.7 1.3 %copy.12 = bf16[8,1024]{1,0:T(8,128)(2,1)} copy(bf16[8,1024]{1,0:T(8,128)(2,1)} %get-tuple-element.8) | data formatting | bytes 32768
  85.0 1.9 %copy.13 = bf16[32,8,1024]{2,1,0:T(8,128)(2,1)} copy(bf16[32,8,1024]{2,1,0:T(8,128)(2,1)} %get-tuple-element.9) | data formatting | bytes 1048576

commit v4 on v2

--- a/solution.py
+++ b/solution.py
@@ -23,38 +23,23 @@
 MSG = 2 * ROWS + 2 * LIST
 
 
-def kernel(
+def radiate(
     n_space,
     n_dirs,
     hist_ref,
     rad_ref,
-    mat_ref,
     w_ref,
-    off_ref,
-    del_ref,
-    src_ref,
-    lag_ref,
-    far_ref,
-    near_ref,
+    recv1,
+    hb,
+    halo,
     hist,
     hq,
-    hb,
-    halo,
     ext,
-    mat,
     rad,
     wz,
     send1,
-    recv1,
-    table,
-    wtab,
-    send2,
-    recv2,
-    padded,
-    acc,
     hist_sem,
     rad_sem,
-    mat_sem,
     w_sem,
     z_send,
     z_recv,
@@ -63,8 +48,6 @@
     own_sem,
     send1_sem,
     recv1_sem,
-    send2_sem,
-    recv2_sem,
 ):
     n_pair = n_space // 4
     per_plane = w_ref.shape[1] // LANES
@@ -113,16 +96,6 @@
             device_id_type=MESH,
         )
 
-    def to_owner(t, slot):
-        return pltpu.make_async_remote_copy(
-            src_ref=send2.at[t],
-            dst_ref=recv2.at[slot],
-            send_sem=send2_sem.at[t],
-            recv_sem=recv2_sem.at[slot],
-            device_id={"space": t},
-            device_id_type=MESH,
-        )
-
     def halo_copy(side):
         return pltpu.make_async_remote_copy(
             src_ref=hb.at[pl.ds(BLK - HB if side == 0 else 0, HB)],
@@ -135,14 +108,12 @@
 
     rows_at = pl.ds(pl.multiple_of(lax.div(plane, 2) * 16, 16), 16)
     hist_copy = pltpu.make_async_copy(hist_ref.at[:, rows_at, :], hist, hist_sem)
-    mat_copy = pltpu.make_async_copy(mat_ref, mat, mat_sem)
     w_copies = [
         pltpu.make_async_copy(
             w_ref.at[:, pl.ds(j * LANES, LANES)], wz.at[plane, j], w_sem.at[j]
         )
         for j in range(per_plane)
     ]
-
     hist_copy.start()
     for copy in w_copies:
         copy.start()
@@ -166,8 +137,6 @@
         return carry
 
     lax.fori_loop(0, n_pair, fetch, 0)
-    mat_copy.start()
-
     hist_copy.wait()
     low_half = lax.rem(plane, 2) == 0
 
@@ -186,6 +155,14 @@
 
     lax.fori_loop(0, TAPS // 2, spread, 0)
     ext[HB : HB + BLK, TAPS : TAPS + QT] = jnp.zeros((BLK, QT, EXC, LANES), jnp.float32)
+
+    for copy in w_copies:
+        copy.wait()
+    pl.semaphore_wait(barrier, n_space - 1 + n_dirs - 1)
+    for i in range(1, n_dirs):
+        z_copy(lax.rem(plane + i, n_dirs)).start()
+    halo_copy(0).start()
+    halo_copy(1).start()
 
     def stack(i, carry):
         for g in range(2):
@@ -203,12 +180,6 @@
         return carry
 
     lax.fori_loop(0, TAPS // 4, stack, 0)
-    for copy in w_copies:
-        copy.wait()
-    pl.semaphore_wait(barrier, n_space - 1 + n_dirs - 1)
-    for i in range(1, n_dirs):
-        z_copy(lax.rem(plane + i, n_dirs)).start()
-
     def aggregate(p):
         for g in range(2):
             rad_copy(p, g).wait()
@@ -252,37 +223,39 @@
 
     lax.fori_loop(1, n_pair, agg_step, 0)
 
-    halo_copy(0).start()
-    halo_copy(1).start()
-
+    def take_in(i, carry):
+        s = lax.rem(me + i, n_space)
+        to_translator(s, s).wait_recv()
+        to_translator(s, me).wait_send()
+        return carry
+
+    lax.fori_loop(1, n_space, take_in, 0)
+    pltpu.make_async_copy(send1.at[me], recv1.at[me], own_sem).wait()
+    for i in range(1, n_dirs):
+        z_copy(lax.rem(plane + i, n_dirs)).wait_send()
+    for side in range(2):
+        halo_copy(side).wait()
+
+
+def translate_near(
+    n_space, recv1, hb, halo, mat, off_ref, del_ref, src_ref, lag_ref, send2, near_ref, table, wtab, ext
+):
+    n_pair = n_space // 4
+    me = lax.axis_index("space")
     table[:, ROWS:SPAN, :] = jnp.zeros((table.shape[0], SPAN - ROWS, LANES), jnp.float32)
-    acc[...] = jnp.zeros_like(acc)
-    padded[:, :, 0:16, :] = jnp.zeros((2, 2, 16, 256), jnp.bfloat16)
-
-    def take_in(i, carry):
-        p = pair_from(i)
-        for j in range(4):
-            s = 4 * p + j
-
-            @pl.when(s != me)
-            def _():
-                to_translator(s, s).wait_recv()
-
-            @pl.when(s == me)
-            def _():
-                pltpu.make_async_copy(send1.at[s], recv1.at[s], own_sem).wait()
-
-            for g in range(2):
-                table[2 * s + g, 0:ROWS, :] = recv1[s, g * ROWS : (g + 1) * ROWS, :].astype(
-                    jnp.float32
-                )
-            wtab[s] = recv1[s, 2 * ROWS : MSG, :].astype(jnp.float32)
-        return carry
-
-    lax.fori_loop(0, n_pair, take_in, 0)
+
+    def take_in(s, carry):
+        for g in range(2):
+            table[2 * s + g, 0:ROWS, :] = recv1[s, g * ROWS : (g + 1) * ROWS, :].astype(
+                jnp.float32
+            )
+        wtab[s] = recv1[s, 2 * ROWS : MSG, :].astype(jnp.float32)
+        return carry
+
+    lax.fori_loop(0, n_space, take_in, 0)
 
     def translate(i, carry):
-        p = pair_at(i)
+        p = i
         for j in range(4):
             t = 4 * p + j
             for g in range(2):
@@ -295,29 +268,21 @@
                         + weights[slot : slot + 1, :] * table[src_ref[slot, 2 * t + g], pl.ds(first, ROWS), :]
                     )
                 send2[t, g * ROWS : (g + 1) * ROWS, :] = total.astype(jnp.bfloat16)
-
-            @pl.when(t != me)
-            def _():
-                to_owner(t, me).start()
-
-            @pl.when(t == me)
-            def _():
-                pltpu.make_async_copy(send2.at[t], recv2.at[t], own_sem).start()
-
         return carry
 
     lax.fori_loop(0, n_pair, translate, 0)
 
-    for side in range(2):
-        halo_copy(side).wait_recv()
-
     def halo_blocks(b, carry):
-        ext[b, 0:TAPS] = halo[0, b].astype(jnp.float32).reshape(TAPS, EXC, LANES)
-        ext[HB + BLK + b, 0:TAPS] = halo[1, b].astype(jnp.float32).reshape(TAPS, EXC, LANES)
+        ext[b] = halo[0, b].astype(jnp.float32).reshape(TAPS, EXC, LANES)
+        ext[HB + BLK + b] = halo[1, b].astype(jnp.float32).reshape(TAPS, EXC, LANES)
         return carry
 
     lax.fori_loop(0, HB, halo_blocks, 0)
-    mat_copy.wait()
+    def own_blocks(b, carry):
+        ext[HB + b] = hb[b].astype(jnp.float32).reshape(TAPS, EXC, LANES)
+        return carry
+
+    lax.fori_loop(0, BLK, own_blocks, 0)
 
     for b in range(BLK):
         near = jnp.zeros((EXC, LANES), jnp.float32)
@@ -335,67 +300,101 @@
             )
         near_ref[:, b * LANES : (b + 1) * LANES] = near.astype(jnp.bfloat16)
 
-    def project(i, carry):
-        p = pair_from(i)
+
+def give_back(n_space, send2, recv2, own_sem, send2_sem, recv2_sem):
+    n_pair = n_space // 4
+    me = lax.axis_index("space")
+    my_pair = lax.div(me, 4)
+
+    def to_owner(t, slot):
+        return pltpu.make_async_remote_copy(
+            src_ref=send2.at[t],
+            dst_ref=recv2.at[slot],
+            send_sem=send2_sem.at[t],
+            recv_sem=recv2_sem.at[slot],
+            device_id={"space": t},
+            device_id_type=MESH,
+        )
+
+    own = pltpu.make_async_copy(send2.at[me], recv2.at[me], own_sem)
+    own.start()
+    barrier = pltpu.get_barrier_semaphore()
+
+    def greet(i, carry):
+        pl.semaphore_signal(
+            barrier, inc=1, device_id={"space": lax.rem(me + i, n_space)}, device_id_type=MESH
+        )
+        return carry
+
+    lax.fori_loop(1, n_space, greet, 0)
+    pl.semaphore_wait(barrier, n_space - 1)
+
+    def post(i, carry):
         for j in range(4):
-            s = 4 * p + j
-
-            @pl.when(s != me)
+            t = 4 * lax.rem(my_pair + i, n_pair) + j
+
+            @pl.when(t != me)
             def _():
-                to_owner(s, s).wait_recv()
-
-            @pl.when(s == me)
-            def _():
-                pltpu.make_async_copy(send2.at[s], recv2.at[s], own_sem).wait()
-
-            jj, c = j // 2, j % 2
+                to_owner(t, me).start()
+
+        return carry
+
+    lax.fori_loop(0, n_pair, post, 0)
+
+    def finish(i, carry):
+        s = lax.rem(me + i, n_space)
+        to_owner(s, s).wait_recv()
+        to_owner(s, me).wait_send()
+        return carry
+
+    lax.fori_loop(1, n_space, finish, 0)
+    own.wait()
+
+
+def project(recv2, rad, far_ref, padded, acc):
+    step = pl.program_id(0)
+
+    @pl.when(step == 0)
+    def _():
+        acc[...] = jnp.zeros_like(acc)
+        padded[:, :, 0:16, :] = jnp.zeros((2, 2, 16, 256), jnp.bfloat16)
+
+    for j in range(4):
+        jj, c = j // 2, j % 2
+        for g in range(2):
+            padded[g, c, 16 : 16 + ROWS, jj * LANES : (jj + 1) * LANES] = recv2[
+                j, g * ROWS : (g + 1) * ROWS, :
+            ]
+    for g in range(2):
+        total = acc[g]
+        for q in range(QT):
+            start = 16 - q * HALF
+            late = jnp.concatenate(
+                [padded[g, c, start : start + ROWS, :] for c in range(2)], axis=0
+            )
+            total = total + lax.dot_general(
+                late,
+                rad[q, g],
+                (((1,), (1,)), ((), ())),
+                preferred_element_type=jnp.float32,
+            )
+        acc[g] = total
+
+    @pl.when(step == pl.num_programs(0) - 1)
+    def _():
+        def finish(a, carry):
             for g in range(2):
-                padded[g, c, 16 : 16 + ROWS, jj * LANES : (jj + 1) * LANES] = recv2[
-                    s, g * ROWS : (g + 1) * ROWS, :
+                halves = [
+                    acc[g, pl.ds(c * ROWS + a * 2 * HALF, 2 * HALF), :] for c in range(2)
                 ]
-        for g in range(2):
-            total = acc[g]
-            for q in range(QT):
-                start = 16 - q * HALF
-                late = jnp.concatenate(
-                    [padded[g, c, start : start + ROWS, :] for c in range(2)], axis=0
-                )
-                total = total + lax.dot_general(
-                    late,
-                    rad[p, g, q],
-                    (((1,), (1,)), ((), ())),
-                    preferred_element_type=jnp.float32,
-                )
-            acc[g] = total
-        return carry
-
-    lax.fori_loop(0, n_pair, project, 0)
-
-    def finish(a, carry):
-        for g in range(2):
-            halves = [
-                acc[g, pl.ds(c * ROWS + a * 2 * HALF, 2 * HALF), :] for c in range(2)
-            ]
-            for i in range(2):
-                rows = [half[i * HALF : (i + 1) * HALF] for half in halves]
-                far_ref[2 * a + i, :, g * GRP : (g + 1) * GRP] = jnp.concatenate(
-                    rows, axis=0
-                ).astype(jnp.bfloat16)
-        return carry
-
-    lax.fori_loop(0, TAPS // 2, finish, 0)
-
-    def drain(i, carry):
-        t = lax.rem(me + i, n_space)
-        to_translator(t, me).wait_send()
-        to_owner(t, me).wait_send()
-        return carry
-
-    lax.fori_loop(1, n_space, drain, 0)
-    for i in range(1, n_dirs):
-        z_copy(lax.rem(plane + i, n_dirs)).wait_send()
-    for side in range(2):
-        halo_copy(side).wait_send()
+                for i in range(2):
+                    rows = [half[i * HALF : (i + 1) * HALF] for half in halves]
+                    far_ref[2 * a + i, :, g * GRP : (g + 1) * GRP] = jnp.concatenate(
+                        rows, axis=0
+                    ).astype(jnp.bfloat16)
+            return carry
+
+        lax.fori_loop(0, TAPS // 2, finish, 0)
 
 
 def local(
@@ -412,41 +411,35 @@
 ):
     cur = history.shape[2]
     dirs = radiation.shape[2]
+    n_pair = n_space // 4
     weights = far_weight.reshape(2 * LIST, -1)
-    n_pair = n_space // 4
+    per_plane = weights.shape[1] // LANES
+    waves = radiation.reshape(QT, 2, GRP, dirs)
     any_spec = pl.BlockSpec(memory_space=pl.ANY)
     smem = pl.BlockSpec(memory_space=pltpu.SMEM)
     vmem = pl.BlockSpec(memory_space=pltpu.VMEM)
     bf16, f32 = jnp.bfloat16, jnp.float32
-    far, near = pl.pallas_call(
-        functools.partial(kernel, n_space, n_dirs),
+    limit = 56 * 1024 * 1024
+    rows = TAPS * EXC
+    recv1, hb, halo = pl.pallas_call(
+        functools.partial(radiate, n_space, n_dirs),
         out_shape=(
-            jax.ShapeDtypeStruct((TAPS, EXC, cur), bf16),
-            jax.ShapeDtypeStruct((EXC, cur), bf16),
+            jax.ShapeDtypeStruct((n_space, MSG, LANES), bf16),
+            jax.ShapeDtypeStruct((BLK, rows, LANES), bf16),
+            jax.ShapeDtypeStruct((2, HB, rows, LANES), bf16),
         ),
-        in_specs=[any_spec] * 4 + [smem] * 4,
-        out_specs=(vmem, vmem),
+        in_specs=[any_spec] * 3,
+        out_specs=(any_spec, vmem, any_spec),
         scratch_shapes=[
             pltpu.VMEM((TAPS, 2 * EXC, cur), bf16),
             pltpu.VMEM((2, 2 * ROWS, QT * GRP), bf16),
-            pltpu.VMEM((BLK, TAPS * EXC, LANES), bf16),
-            pltpu.VMEM((2, HB, TAPS * EXC, LANES), bf16),
             pltpu.VMEM((BLK + 2 * HB, TAPS + QT, EXC, LANES), f32),
-            pltpu.VMEM(near_matrix.shape, bf16),
             pltpu.VMEM((n_pair, 2, QT, GRP, 256), bf16),
-            pltpu.VMEM((n_dirs, weights.shape[1] // LANES, 2 * LIST, LANES), bf16),
+            pltpu.VMEM((n_dirs, per_plane, 2 * LIST, LANES), bf16),
             pltpu.VMEM((n_space, MSG, LANES), bf16),
-            pltpu.VMEM((n_space, MSG, LANES), bf16),
-            pltpu.VMEM((2 * n_space, SPAN, LANES), f32),
-            pltpu.VMEM((n_space, 2 * LIST, LANES), f32),
-            pltpu.VMEM((n_space, 2 * ROWS, LANES), bf16),
-            pltpu.VMEM((n_space, 2 * ROWS, LANES), bf16),
-            pltpu.VMEM((2, 2, 16 + ROWS, 256), bf16),
-            pltpu.VMEM((2, 2 * ROWS, GRP), f32),
             pltpu.SemaphoreType.DMA,
             pltpu.SemaphoreType.DMA((n_pair, 2)),
-            pltpu.SemaphoreType.DMA,
-            pltpu.SemaphoreType.DMA((weights.shape[1] // LANES,)),
+            pltpu.SemaphoreType.DMA((per_plane,)),
             pltpu.SemaphoreType.DMA((n_dirs,)),
             pltpu.SemaphoreType.DMA((n_dirs,)),
             pltpu.SemaphoreType.DMA((2,)),
@@ -454,27 +447,55 @@
             pltpu.SemaphoreType.DMA,
             pltpu.SemaphoreType.DMA((n_space,)),
             pltpu.SemaphoreType.DMA((n_space,)),
+        ],
+        compiler_params=pltpu.CompilerParams(
+            collective_id=0, has_side_effects=True, vmem_limit_bytes=limit
+        ),
+    )(history, waves, weights)
+    send2, near = pl.pallas_call(
+        functools.partial(translate_near, n_space),
+        out_shape=(
+            jax.ShapeDtypeStruct((n_space, 2 * ROWS, LANES), bf16),
+            jax.ShapeDtypeStruct((EXC, cur), bf16),
+        ),
+        in_specs=[vmem] * 4 + [smem] * 4,
+        out_specs=(vmem, vmem),
+        scratch_shapes=[
+            pltpu.VMEM((2 * n_space, SPAN, LANES), f32),
+            pltpu.VMEM((n_space, 2 * LIST, LANES), f32),
+            pltpu.VMEM((BLK + 2 * HB, TAPS, EXC, LANES), f32),
+        ],
+        compiler_params=pltpu.CompilerParams(vmem_limit_bytes=limit),
+    )(recv1, hb, halo, near_matrix, near_offset, near_delay, far_source.T, far_delay.T)
+    recv2 = pl.pallas_call(
+        functools.partial(give_back, n_space),
+        out_shape=jax.ShapeDtypeStruct((n_space, 2 * ROWS, LANES), bf16),
+        in_specs=[any_spec],
+        out_specs=any_spec,
+        scratch_shapes=[
+            pltpu.SemaphoreType.DMA,
             pltpu.SemaphoreType.DMA((n_space,)),
             pltpu.SemaphoreType.DMA((n_space,)),
         ],
         compiler_params=pltpu.CompilerParams(
-            collective_id=0, has_side_effects=True, vmem_limit_bytes=56 * 1024 * 1024
+            collective_id=1, has_side_effects=True, vmem_limit_bytes=limit
         ),
-        cost_estimate=pl.CostEstimate(
-            flops=8 * QT * TAPS * EXC * cur * dirs // 2,
-            bytes_accessed=2 * QT * cur * dirs,
-            transcendentals=0,
-        ),
-    )(
-        history,
-        radiation.reshape(QT, 2, GRP, dirs),
-        near_matrix,
-        weights,
-        near_offset,
-        near_delay,
-        far_source.T,
-        far_delay.T,
-    )
+    )(send2)
+    far = pl.pallas_call(
+        project,
+        grid=(n_pair,),
+        out_shape=jax.ShapeDtypeStruct((TAPS, EXC, cur), bf16),
+        in_specs=[
+            pl.BlockSpec((4, 2 * ROWS, LANES), lambda i: (i, 0, 0)),
+            pl.BlockSpec((QT, 2, GRP, 256), lambda i: (0, 0, 0, i)),
+        ],
+        out_specs=pl.BlockSpec((TAPS, EXC, cur), lambda i: (0, 0, 0)),
+        scratch_shapes=[
+            pltpu.VMEM((2, 2, 16 + ROWS, 256), bf16),
+            pltpu.VMEM((2, 2 * ROWS, GRP), f32),
+        ],
+        compiler_params=pltpu.CompilerParams(vmem_limit_bytes=limit),
+    )(recv2, waves)
     return near, far
 
 

time: 86.1 us -> 101 us (1.17)
  Pallas kernels: 82 us -> 99.7 us
  local copies, waits for them, and re-layouts: 3.19 us -> 0 us
    pallas_call x1 -> x4, Pallas kernels: 82 us -> 99.7 us  [the longest x1 45.5 us: local(): pl.pallas_call(functools.partial(radiate, n_space, n_dirs), out_shape=(ja...]
    unnamed x2 -> x0, local copies, waits for them, and re-layouts: 3.19 us -> none
where the time goes in v4:
time: 101 us; the launch traced here: 100 us
  Pallas kernels  99.7 us (99%)
    pallas_call x1, Pallas kernels, local(): pl.pallas_call(functools.partial(radiate, n_space, n_dirs), out_shape=(ja...  45.5 us
    pallas_call x1, Pallas kernels, local(): pl.pallas_call(functools.partial(give_back, n_space), out_shape=jax.Shape...  33.8 us
    pallas_call x1, Pallas kernels, local(): pl.pallas_call(project, grid=(n_pair,), out_shape=jax.ShapeDtypeStruct((T...  12 us
    pallas_call x1, Pallas kernels, local(): pl.pallas_call(functools.partial(translate_near, n_space), out_shape=(jax...  8.37 us

profile of v4, /device:TPU:1, one launch (start us, length us, event | category | flops | bytes accessed | tf_op | source)
XLA Modules:
  0.0 100.3 jit_solution(7685663720278178570)
XLA Ops:
  0.6 45.5 %shard_map.95 = (bf16[32,272,128]{2,1,0:T(8,128)(2,1)}, bf16[8,256,128]{2,1,0:T(8,128)(2,1)}, bf16[2,4,256,128]{3,2,1,0:T(8,128)(2,1)}) custom-call(bf16[32,32,1024]{2,1,0:T(8,128)(2,1)} %hist_ref.1, bf16[4,2,512,2048]{3,2,1,0:T(8,128)(2,1)} %bitcast.4, bf16[16,512]{1,0:T(8,128)(2,1)} %bitcast.6), custom_call_target="tpu_custom_call" | custom-call | tf_op jit(solution)/shard_map/pallas_call | solution.py:424
  46.1 8.4 %shard_map.96 = (bf16[32,256,128]{2,1,0:T(8,128)(2,1)}, bf16[8,1024]{1,0:T(8,128)(2,1)}) custom-call(bf16[32,272,128]{2,1,0:T(8,128)(2,1)} %get-tuple-element.7.recv1, bf16[8,256,128]{2,1,0:T(8,128)(2,1)} %get-tuple-element.8.hb, bf16[2,4,256,128]{3,2,1,0:T(8,128)(2,1)} %get-tuple-element.9.halo, bf16[8,8,128,128]{3,2,1,0:T(8,128)(2,1)} %mat.1, ...), custom_call_target="tpu_custom_call" | custom-call | tf_op jit(solution)/shard_map/pallas_call | solution.py:455
  54.5 33.8 %shard_map.97.recv2 = bf16[32,256,128]{2,1,0:T(8,128)(2,1)} custom-call(bf16[32,256,128]{2,1,0:T(8,128)(2,1)} %get-tuple-element.11.send2), custom_call_target="tpu_custom_call" | custom-call | tf_op jit(solution)/shard_map/pallas_call | solution.py:470
  88.3 12.0 %shard_map.98 = bf16[32,8,1024]{2,1,0:T(8,128)(2,1)} custom-call(bf16[32,256,128]{2,1,0:T(8,128)(2,1)} %shard_map.97.recv2, bf16[4,2,512,2048]{3,2,1,0:T(8,128)(2,1)} %bitcast.5), custom_call_target="tpu_custom_call" | custom-call | tf_op jit(solution)/shard_map/pallas_call | solution.py:484

commit v5 on v3

--- a/solution.py
+++ b/solution.py
@@ -23,7 +23,8 @@
 MSG = 2 * ROWS + 2 * LIST
 SIDE = 4
 TIES = ((2, 2), (1, 2), (3, 2), (0, 2), (2, 3), (2, 0), (2, 1))
-N_RELAY = 4 * len(TIES)
+N_RELAY = 2 * len(TIES)
+BY = 80
 
 
 def kernel(
@@ -88,7 +89,7 @@
         return (lax.rem(y, SIDE) * SIDE + lax.rem(x, SIDE)) * 2 + c
 
     def pair_at(i):
-        y = lax.rem(my_y + 2 + lax.div(i, 2), SIDE)
+        y = lax.rem(my_y + 2 + (1 + 2 * my_core) * lax.div(i, 2), SIDE)
         half = lax.rem(lax.div(my_x, 2) + 1 + i, 2)
         return 2 * y + half
 
@@ -102,8 +103,8 @@
         dy = lax.rem(lax.div(t, 2 * SIDE) + SIDE - my_y, SIDE)
         return dx, dy, jnp.logical_or(dx == 2, dy == 2)
 
-    def half_rows(h, rows):
-        return pl.ds(0, ROWS) if h == 0 else pl.ds(ROWS, rows - ROWS)
+    def part_rows(h, rows):
+        return pl.ds(0, rows - BY) if h == 0 else pl.ds(rows - BY, BY)
 
     def remote(src, dst, send, recv, t):
         return pltpu.make_async_remote_copy(
@@ -124,9 +125,9 @@
         rows, send, recv, _, send_sem, recv_sem, _, _ = exchanges[ex]
         return remote(send.at[t], recv.at[slot], send_sem.at[t, 0], recv_sem.at[slot, 0], t)
 
-    def half(ex, t, slot, h):
+    def piece(ex, t, slot, h):
         rows, send, recv, _, send_sem, recv_sem, _, _ = exchanges[ex]
-        at = half_rows(h, rows)
+        at = part_rows(h, rows)
         return remote(
             send.at[t, at], recv.at[slot, at], send_sem.at[t, h], recv_sem.at[slot, h], t
         )
@@ -149,30 +150,29 @@
             along_y = jnp.where(dy == 2, 1, 0)
             first = jnp.where(dx == 0, 3, jnp.where(dx == 1, 1, jnp.where(dx == 3, 2, 0)))
             kind = jnp.where(dy == 2, first, 4 + lax.rem(dy + 1, SIDE))
-            for h in range(2):
-                turn = 1 if h == 0 else SIDE - 1
-                by = device(my_x + turn * along_x, my_y + turn * along_y, lax.rem(t, 2))
-                slot = kind * 4 + 2 * h + my_core
-                at = half_rows(h, rows)
-                remote(
-                    send.at[t, at],
-                    relay.at[slot, pl.ds(0, at.size)],
-                    send_sem.at[t, h],
-                    relay_sem.at[slot],
-                    by,
-                ).start()
+            by = device(my_x + SIDE - along_x, my_y + SIDE - along_y, lax.rem(t, 2))
+            slot = kind * 2 + my_core
+            remote(
+                send.at[t, part_rows(1, rows)],
+                relay.at[slot],
+                send_sem.at[t, 1],
+                relay_sem.at[slot],
+                by,
+            ).start()
+            piece(ex, t, me, 0).start()
 
     def pass_on(ex, slot, start):
         rows, send, recv, relay, _, recv_sem, relay_sem, forward_sem = exchanges[ex]
-        (dx, dy), h, c = TIES[slot // 4], slot // 2 % 2, slot % 2
-        back = SIDE - 1 if h == 0 else 1
-        x = my_x + back * (dx == 2)
-        y = my_y + back * (dy == 2)
+        (dx, dy), c = TIES[slot // 2], slot % 2
+        x, y = my_x + (dx == 2), my_y + (dy == 2)
         sender, target = device(x, y, c), device(x + dx, y + dy, my_core)
-        at = half_rows(h, rows)
-        held = relay.at[slot, pl.ds(0, at.size)]
+        held = relay.at[slot]
         onward = remote(
-            held, recv.at[sender, at], forward_sem.at[slot], recv_sem.at[sender, h], target
+            held,
+            recv.at[sender, part_rows(1, rows)],
+            forward_sem.at[slot],
+            recv_sem.at[sender, 1],
+            target,
         )
         if start:
             remote(held, held, forward_sem.at[slot], relay_sem.at[slot], target).wait_recv()
@@ -195,7 +195,7 @@
         @pl.when(tie)
         def _():
             for h in range(2):
-                half(ex, s, s, h).wait_recv()
+                piece(ex, s, s, h).wait_recv()
 
     def sent(ex, t):
         tie = steps_to(t)[2]
@@ -207,7 +207,7 @@
         @pl.when(tie)
         def _():
             for h in range(2):
-                half(ex, t, me, h).wait_send()
+                piece(ex, t, me, h).wait_send()
 
     def rad_copy(p, g):
         cols = pl.ds(pl.multiple_of(p * 256, 256), 256)
@@ -483,6 +483,17 @@
         z_copy(lax.rem(plane + i, n_dirs)).wait_send()
     for side in range(2):
         halo_copy(side).wait_send()
+
+
+def copy_out(far_ref, near_ref, far_out, near_out, sems):
+    copies = [
+        pltpu.make_async_copy(far_ref, far_out, sems.at[0]),
+        pltpu.make_async_copy(near_ref, near_out, sems.at[1]),
+    ]
+    for copy in copies:
+        copy.start()
+    for copy in copies:
+        copy.wait()
 
 
 def local(
@@ -528,8 +539,8 @@
             pltpu.VMEM((n_space, 2 * LIST, LANES), f32),
             pltpu.VMEM((n_space, 2 * ROWS, LANES), bf16),
             pltpu.VMEM((n_space, 2 * ROWS, LANES), bf16),
-            pltpu.VMEM((N_RELAY, MSG - ROWS, LANES), bf16),
-            pltpu.VMEM((N_RELAY, ROWS, LANES), bf16),
+            pltpu.VMEM((N_RELAY, BY, LANES), bf16),
+            pltpu.VMEM((N_RELAY, BY, LANES), bf16),
             pltpu.VMEM((2, 2, 16 + ROWS, 256), bf16),
             pltpu.VMEM((2, 2 * ROWS, GRP), f32),
             pltpu.SemaphoreType.DMA,
@@ -568,6 +579,17 @@
         far_source.T,
         far_delay.T,
     )
+    far, near = pl.pallas_call(
+        copy_out,
+        out_shape=(
+            jax.ShapeDtypeStruct(far.shape, bf16),
+            jax.ShapeDtypeStruct(near.shape, bf16),
+        ),
+        in_specs=[any_spec] * 2,
+        out_specs=(any_spec, any_spec),
+        scratch_shapes=[pltpu.SemaphoreType.DMA((2,))],
+        compiler_params=pltpu.CompilerParams(vmem_limit_bytes=56 * 1024 * 1024),
+    )(far, near)
     return near, far
 
 

time: 87.1 us -> 101 us (1.16)
  the two profiles are of different devices: /device:TPU:2 before, /device:TPU:1 now
where the time goes in v5:
time: 101 us; the launch traced here: 99.2 us
  Pallas kernels  98.6 us (98%)
    pallas_call x1, Pallas kernels, local(): pl.pallas_call(functools.partial(kernel, n_space, n_dirs), out_shape=(jax...  81.1 us
    pallas_call x1, Pallas kernels, local(): pl.pallas_call(copy_out, out_shape=(jax.ShapeDtypeStruct(far.shape, bf16)...  17.5 us

profile of v5, /device:TPU:1, one launch (start us, length us, event | category | flops | bytes accessed | tf_op | source)
XLA Modules:
  0.0 99.2 jit_solution(1769302104265324365)
XLA Ops:
  0.6 81.1 %shard_map.95 = (bf16[32,8,1024]{2,1,0:T(8,128)(2,1)}, bf16[8,1024]{1,0:T(8,128)(2,1)}) custom-call(bf16[32,32,1024]{2,1,0:T(8,128)(2,1)} %hist_ref.1, bf16[4,2,512,2048]{3,2,1,0:T(8,128)(2,1)} %bitcast.4, bf16[8,8,128,128]{3,2,1,0:T(8,128)(2,1)} %mat_ref.1, bf16[16,512]{1,0:T(8,128)(2,1)} %bitcast.5, s32[8,8]{1,0:T(8,128)} %off_ref.1, s32[8,8]{1,0:T(8,128)} %del_ref.1, ...), custom_call_target="tpu_custom_call" | custom-call | flops 8589934592 | bytes 16777216 | tf_op jit(solution)/shard_map/pallas_call | solution.py:519
  81.7 17.5 %shard_map.96 = (bf16[32,8,1024]{2,1,0:T(8,128)(2,1)}, bf16[8,1024]{1,0:T(8,128)(2,1)}) custom-call(bf16[32,8,1024]{2,1,0:T(8,128)(2,1)} %get-tuple-element.6.far_ref, bf16[8,1024]{1,0:T(8,128)(2,1)} %get-tuple-element.7.near_ref), custom_call_target="tpu_custom_call" | custom-call | tf_op jit(solution)/shard_map/pallas_call | solution.py:582

commit v6 on v2

--- a/solution.py
+++ b/solution.py
@@ -20,7 +20,6 @@
 ROWS = TAPS * HALF
 SPAN = ROWS + 16 * HALF
 GRP = 512
-MSG = 2 * ROWS + 2 * LIST
 
 
 def kernel(
@@ -43,7 +42,8 @@
     ext,
     mat,
     rad,
-    wz,
+    wq,
+    wall,
     send1,
     recv1,
     table,
@@ -56,8 +56,11 @@
     rad_sem,
     mat_sem,
     w_sem,
-    z_send,
-    z_recv,
+    wq_send,
+    wq_recv,
+    wq_own,
+    wall_send,
+    wall_recv,
     halo_send,
     halo_recv,
     own_sem,
@@ -83,25 +86,40 @@
         cols = pl.ds(pl.multiple_of(p * 256, 256), 256)
         return pltpu.make_async_copy(rad_ref.at[:, g, :, cols], rad.at[p, g], rad_sem.at[p, g])
 
-    def z_copy(to):
+    def weight_copy(j, c, slot):
+        chip = plane * per_plane + j
         return pltpu.make_async_remote_copy(
-            src_ref=wz.at[plane],
-            dst_ref=wz.at[plane],
-            send_sem=z_send.at[to],
-            recv_sem=z_recv.at[plane],
+            src_ref=wq.at[j],
+            dst_ref=wall.at[slot],
+            send_sem=wq_send.at[j, c],
+            recv_sem=wq_recv.at[slot],
+            device_id={"space": 2 * chip + c},
+            device_id_type=MESH,
+        )
+
+    def weights_up(to):
+        return pltpu.make_async_remote_copy(
+            src_ref=wall,
+            dst_ref=wall,
+            send_sem=wall_send.at[to],
+            recv_sem=wall_recv,
             device_id={"dirs": to},
             device_id_type=MESH,
         )
 
-    def z_arrival(frm):
-        return pltpu.make_async_remote_copy(
-            src_ref=wz.at[frm],
-            dst_ref=wz.at[frm],
-            send_sem=z_send.at[frm],
-            recv_sem=z_recv.at[frm],
-            device_id={"dirs": frm},
-            device_id_type=MESH,
-        )
+    my_chip = lax.div(me, 2)
+    home = lax.div(my_chip, per_plane)
+    own_weights = pltpu.make_async_copy(
+        wq.at[lax.rem(my_chip, per_plane)], wall.at[me], wq_own
+    )
+
+    def each_weight(act):
+        for j in range(per_plane):
+            for c in range(2):
+
+                @pl.when(2 * (plane * per_plane + j) + c != me)
+                def _():
+                    act(weight_copy(j, c, me))
 
     def to_translator(t, slot):
         return pltpu.make_async_remote_copy(
@@ -138,7 +156,7 @@
     mat_copy = pltpu.make_async_copy(mat_ref, mat, mat_sem)
     w_copies = [
         pltpu.make_async_copy(
-            w_ref.at[:, pl.ds(j * LANES, LANES)], wz.at[plane, j], w_sem.at[j]
+            w_ref.at[:, pl.ds(j * LANES, LANES)], wq.at[j], w_sem.at[j]
         )
         for j in range(per_plane)
     ]
@@ -203,11 +221,6 @@
         return carry
 
     lax.fori_loop(0, TAPS // 4, stack, 0)
-    for copy in w_copies:
-        copy.wait()
-    pl.semaphore_wait(barrier, n_space - 1 + n_dirs - 1)
-    for i in range(1, n_dirs):
-        z_copy(lax.rem(plane + i, n_dirs)).start()
 
     def aggregate(p):
         for g in range(2):
@@ -225,11 +238,8 @@
 
     def dispatch(p):
         for jj in range(2):
-            chip = 2 * p + jj
-            weights = wz[lax.div(chip, per_plane), lax.rem(chip, per_plane)]
             for c in range(2):
                 t = 4 * p + 2 * jj + c
-                send1[t, pl.ds(2 * ROWS, 2 * LIST), :] = weights
 
                 @pl.when(t != me)
                 def _():
@@ -240,9 +250,17 @@
                     pltpu.make_async_copy(send1.at[t], recv1.at[t], own_sem).start()
 
     aggregate(my_pair)
-    for i in range(1, n_dirs):
-        z_arrival(lax.rem(plane + n_dirs - i, n_dirs)).wait_recv()
+    for copy in w_copies:
+        copy.wait()
+    pl.semaphore_wait(barrier, n_space - 1 + n_dirs - 1)
     dispatch(my_pair)
+    halo_copy(0).start()
+    halo_copy(1).start()
+    each_weight(lambda copy: copy.start())
+
+    @pl.when(plane == home)
+    def _():
+        own_weights.start()
 
     def agg_step(i, carry):
         p = pair_at(i)
@@ -252,8 +270,17 @@
 
     lax.fori_loop(1, n_pair, agg_step, 0)
 
-    halo_copy(0).start()
-    halo_copy(1).start()
+    @pl.when(plane == home)
+    def _():
+        own_weights.wait()
+
+        def gather(i, carry):
+            weight_copy(0, 0, lax.rem(me + i, n_space)).wait_recv()
+            return carry
+
+        lax.fori_loop(1, n_space, gather, 0)
+        for i in range(1, n_dirs):
+            weights_up(lax.rem(plane + i, n_dirs)).start()
 
     table[:, ROWS:SPAN, :] = jnp.zeros((table.shape[0], SPAN - ROWS, LANES), jnp.float32)
     acc[...] = jnp.zeros_like(acc)
@@ -276,9 +303,13 @@
                 table[2 * s + g, 0:ROWS, :] = recv1[s, g * ROWS : (g + 1) * ROWS, :].astype(
                     jnp.float32
                 )
-            wtab[s] = recv1[s, 2 * ROWS : MSG, :].astype(jnp.float32)
-        return carry
-
+        return carry
+
+    @pl.when(plane != home)
+    def _():
+        weights_up(home).wait_recv()
+
+    wtab[...] = wall[...].astype(jnp.float32)
     lax.fori_loop(0, n_pair, take_in, 0)
 
     def translate(i, carry):
@@ -392,10 +423,20 @@
         return carry
 
     lax.fori_loop(1, n_space, drain, 0)
-    for i in range(1, n_dirs):
-        z_copy(lax.rem(plane + i, n_dirs)).wait_send()
+    each_weight(lambda copy: copy.wait_send())
+
+    @pl.when(plane == home)
+    def _():
+        for i in range(1, n_dirs):
+            weights_up(lax.rem(plane + i, n_dirs)).wait_send()
+
     for side in range(2):
         halo_copy(side).wait_send()
+
+
+def hand_out(far_ref, near_ref, far_out, near_out):
+    far_out[...] = far_ref[...]
+    near_out[...] = near_ref[...]
 
 
 def local(
@@ -434,9 +475,10 @@
             pltpu.VMEM((BLK + 2 * HB, TAPS + QT, EXC, LANES), f32),
             pltpu.VMEM(near_matrix.shape, bf16),
             pltpu.VMEM((n_pair, 2, QT, GRP, 256), bf16),
-            pltpu.VMEM((n_dirs, weights.shape[1] // LANES, 2 * LIST, LANES), bf16),
-            pltpu.VMEM((n_space, MSG, LANES), bf16),
-            pltpu.VMEM((n_space, MSG, LANES), bf16),
+            pltpu.VMEM((weights.shape[1] // LANES, 2 * LIST, LANES), bf16),
+            pltpu.VMEM((n_space, 2 * LIST, LANES), bf16),
+            pltpu.VMEM((n_space, 2 * ROWS, LANES), bf16),
+            pltpu.VMEM((n_space, 2 * ROWS, LANES), bf16),
             pltpu.VMEM((2 * n_space, SPAN, LANES), f32),
             pltpu.VMEM((n_space, 2 * LIST, LANES), f32),
             pltpu.VMEM((n_space, 2 * ROWS, LANES), bf16),
@@ -447,8 +489,11 @@
             pltpu.SemaphoreType.DMA((n_pair, 2)),
             pltpu.SemaphoreType.DMA,
             pltpu.SemaphoreType.DMA((weights.shape[1] // LANES,)),
+            pltpu.SemaphoreType.DMA((weights.shape[1] // LANES, 2)),
+            pltpu.SemaphoreType.DMA((n_space,)),
+            pltpu.SemaphoreType.DMA,
             pltpu.SemaphoreType.DMA((n_dirs,)),
-            pltpu.SemaphoreType.DMA((n_dirs,)),
+            pltpu.SemaphoreType.DMA,
             pltpu.SemaphoreType.DMA((2,)),
             pltpu.SemaphoreType.DMA((2,)),
             pltpu.SemaphoreType.DMA,
@@ -475,6 +520,16 @@
         far_source.T,
         far_delay.T,
     )
+    far, near = pl.pallas_call(
+        hand_out,
+        out_shape=(
+            jax.ShapeDtypeStruct(far.shape, bf16),
+            jax.ShapeDtypeStruct(near.shape, bf16),
+        ),
+        in_specs=[vmem] * 2,
+        out_specs=(vmem, vmem),
+        compiler_params=pltpu.CompilerParams(vmem_limit_bytes=56 * 1024 * 1024),
+    )(far, near)
     return near, far
 
 

time: 86.1 us -> 78.7 us (0.914)
  Pallas kernels: 82 us -> 77.9 us
  local copies, waits for them, and re-layouts: 3.19 us -> 0 us
    pallas_call x1, Pallas kernels: 82 us -> 76 us  [local(): pl.pallas_call(functools.partial(kernel, n_space, n_dirs), out_shape=(jax...]
    unnamed x2 -> x0, local copies, waits for them, and re-layouts: 3.19 us -> none
    pallas_call x0 -> x1, Pallas kernels: none -> 1.87 us  [local(): pl.pallas_call(hand_out, out_shape=(jax.ShapeDtypeStruct(far.shape, bf16)...]
where the time goes in v6:
time: 78.7 us; the launch traced here: 78.5 us
  Pallas kernels  77.9 us (99%)
    pallas_call x1, Pallas kernels, local(): pl.pallas_call(functools.partial(kernel, n_space, n_dirs), out_shape=(jax...  76 us
    pallas_call x1, Pallas kernels, local(): pl.pallas_call(hand_out, out_shape=(jax.ShapeDtypeStruct(far.shape, bf16)...  1.87 us

profile of v6, /device:TPU:1, one launch (start us, length us, event | category | flops | bytes accessed | tf_op | source)
XLA Modules:
  0.0 78.5 jit_solution(7975817450667401275)
XLA Ops:
  0.6 76.0 %shard_map.95 = (bf16[32,8,1024]{2,1,0:T(8,128)(2,1)}, bf16[8,1024]{1,0:T(8,128)(2,1)}) custom-call(bf16[32,32,1024]{2,1,0:T(8,128)(2,1)} %hist_ref.1, bf16[4,2,512,2048]{3,2,1,0:T(8,128)(2,1)} %bitcast.4, bf16[8,8,128,128]{3,2,1,0:T(8,128)(2,1)} %mat_ref.1, bf16[16,512]{1,0:T(8,128)(2,1)} %bitcast.5, s32[8,8]{1,0:T(8,128)} %off_ref.1, s32[8,8]{1,0:T(8,128)} %del_ref.1, ...), custom_call_target="tpu_custom_call" | custom-call | flops 8589934592 | bytes 16777216 | tf_op jit(solution)/shard_map/pallas_call | solution.py:462
  76.7 1.9 %shard_map.96 = (bf16[32,8,1024]{2,1,0:T(8,128)(2,1)}, bf16[8,1024]{1,0:T(8,128)(2,1)}) custom-call(bf16[32,8,1024]{2,1,0:T(8,128)(2,1)} %get-tuple-element.6.far_ref, bf16[8,1024]{1,0:T(8,128)(2,1)} %get-tuple-element.7.near_ref), custom_call_target="tpu_custom_call" | custom-call | tf_op jit(solution)/shard_map/pallas_call | solution.py:523

commit v7 on v6

--- a/solution.py
+++ b/solution.py
@@ -76,11 +76,20 @@
     my_pair = lax.div(me, 4)
     right, left = lax.rem(me + 1, n_space), lax.rem(me + n_space - 1, n_space)
 
+    my_core = lax.rem(me, 2)
+    middle = max(n_pair // 2, 1)
+
     def pair_at(i):
-        return lax.rem(my_pair + i, n_pair)
+        return lax.rem(my_pair + (1 + my_core * (n_pair - 2)) * i, n_pair)
 
     def pair_from(i):
-        return lax.rem(my_pair + n_pair - i, n_pair)
+        odd = lax.rem(i, 2)
+        even_step = lax.rem(middle - lax.div(i, 2) + middle, middle)
+        odd_step = middle + lax.div(i, 2)
+        return lax.rem(my_pair + odd * odd_step + (1 - odd) * even_step, n_pair)
+
+    def target(p, j):
+        return 4 * p + lax.rem(j + me, 4)
 
     def rad_copy(p, g):
         cols = pl.ds(pl.multiple_of(p * 256, 256), 256)
@@ -237,17 +246,16 @@
                     ]
 
     def dispatch(p):
-        for jj in range(2):
-            for c in range(2):
-                t = 4 * p + 2 * jj + c
-
-                @pl.when(t != me)
-                def _():
-                    to_translator(t, me).start()
-
-                @pl.when(t == me)
-                def _():
-                    pltpu.make_async_copy(send1.at[t], recv1.at[t], own_sem).start()
+        for j in range(4):
+            t = target(p, j)
+
+            @pl.when(t != me)
+            def _():
+                to_translator(t, me).start()
+
+            @pl.when(t == me)
+            def _():
+                pltpu.make_async_copy(send1.at[t], recv1.at[t], own_sem).start()
 
     aggregate(my_pair)
     for copy in w_copies:
@@ -315,7 +323,7 @@
     def translate(i, carry):
         p = pair_at(i)
         for j in range(4):
-            t = 4 * p + j
+            t = target(p, j)
             for g in range(2):
                 weights = wtab[t, g * LIST : (g + 1) * LIST, :]
                 total = jnp.zeros((ROWS, LANES), jnp.float32)

time: 78.7 us -> 75.5 us (0.959)
  Pallas kernels: 77.9 us -> 74.7 us
    pallas_call x1, Pallas kernels: 76 us -> 72.8 us  [local(): pl.pallas_call(functools.partial(kernel, n_space, n_dirs), out_shape=(jax...]
where the time goes in v7:
time: 75.5 us; the launch traced here: 75.4 us
  Pallas kernels  74.7 us (99%)
    pallas_call x1, Pallas kernels, local(): pl.pallas_call(functools.partial(kernel, n_space, n_dirs), out_shape=(jax...  72.8 us
    pallas_call x1, Pallas kernels, local(): pl.pallas_call(hand_out, out_shape=(jax.ShapeDtypeStruct(far.shape, bf16)...  1.87 us

profile of v7, /device:TPU:1, one launch (start us, length us, event | category | flops | bytes accessed | tf_op | source)
XLA Modules:
  0.0 75.4 jit_solution(7058777536121087182)
XLA Ops:
  0.6 72.8 %shard_map.95 = (bf16[32,8,1024]{2,1,0:T(8,128)(2,1)}, bf16[8,1024]{1,0:T(8,128)(2,1)}) custom-call(bf16[32,32,1024]{2,1,0:T(8,128)(2,1)} %hist_ref.1, bf16[4,2,512,2048]{3,2,1,0:T(8,128)(2,1)} %bitcast.4, bf16[8,8,128,128]{3,2,1,0:T(8,128)(2,1)} %mat_ref.1, bf16[16,512]{1,0:T(8,128)(2,1)} %bitcast.5, s32[8,8]{1,0:T(8,128)} %off_ref.1, s32[8,8]{1,0:T(8,128)} %del_ref.1, ...), custom_call_target="tpu_custom_call" | custom-call | flops 8589934592 | bytes 16777216 | tf_op jit(solution)/shard_map/pallas_call | solution.py:470
  73.5 1.9 %shard_map.96 = (bf16[32,8,1024]{2,1,0:T(8,128)(2,1)}, bf16[8,1024]{1,0:T(8,128)(2,1)}) custom-call(bf16[32,8,1024]{2,1,0:T(8,128)(2,1)} %get-tuple-element.6.far_ref, bf16[8,1024]{1,0:T(8,128)(2,1)} %get-tuple-element.7.near_ref), custom_call_target="tpu_custom_call" | custom-call | tf_op jit(solution)/shard_map/pallas_call | solution.py:531

commit v8 on v7

--- a/solution.py
+++ b/solution.py
@@ -20,6 +20,9 @@
 ROWS = TAPS * HALF
 SPAN = ROWS + 16 * HALF
 GRP = 512
+
+
+SIDE = 4
 
 
 def kernel(
@@ -51,6 +54,7 @@
     send2,
     recv2,
     padded,
+    lhs,
     acc,
     hist_sem,
     rad_sem,
@@ -73,27 +77,43 @@
     per_plane = w_ref.shape[1] // LANES
     me = lax.axis_index("space")
     plane = lax.axis_index("dirs")
-    my_pair = lax.div(me, 4)
     right, left = lax.rem(me + 1, n_space), lax.rem(me + n_space - 1, n_space)
 
     my_core = lax.rem(me, 2)
-    middle = max(n_pair // 2, 1)
+    n_row = n_space // (2 * SIDE)
+    my_x = lax.rem(lax.div(me, 2), SIDE)
+    my_y = lax.div(me, 2 * SIDE)
+
+    def step_of(i):
+        inner = jnp.logical_and(i >= 2, i < 6)
+        dy = jnp.where(inner, 2 * lax.rem(i, 2), jnp.where(i < 2, 1, 3))
+        other = jnp.where(inner, lax.div(i - 2, 2), lax.rem(i, 2))
+        return dy, other
+
+    def pair_of(dy, other):
+        return 2 * lax.rem(my_y + dy, n_row) + lax.rem(lax.div(my_x, 2) + other, 2)
 
     def pair_at(i):
-        return lax.rem(my_pair + (1 + my_core * (n_pair - 2)) * i, n_pair)
+        dy, other = step_of(i)
+        return pair_of(dy + my_core * (SIDE - 2 * dy), other)
 
     def pair_from(i):
-        odd = lax.rem(i, 2)
-        even_step = lax.rem(middle - lax.div(i, 2) + middle, middle)
-        odd_step = middle + lax.div(i, 2)
-        return lax.rem(my_pair + odd * odd_step + (1 - odd) * even_step, n_pair)
+        dy, other = step_of(lax.rem(i + 2, n_pair))
+        return pair_of(dy, other)
 
     def target(p, j):
-        return 4 * p + lax.rem(j + me, 4)
-
-    def rad_copy(p, g):
+        own = lax.rem(p, 2) == lax.div(my_x, 2)
+        near = lax.rem(my_x + jnp.where(own, 0, 1), 2)
+        column = lax.rem(near + j // 2, 2)
+        return 4 * p + 2 * column + lax.rem(my_core + j, 2)
+
+    def rad_copy(p, g, q):
         cols = pl.ds(pl.multiple_of(p * 256, 256), 256)
-        return pltpu.make_async_copy(rad_ref.at[:, g, :, cols], rad.at[p, g], rad_sem.at[p, g])
+        return pltpu.make_async_copy(
+            rad_ref.at[q, g, :, cols],
+            rad.at[p, g, :, pl.ds(q * 256, 256)],
+            rad_sem.at[p, g, q],
+        )
 
     def weight_copy(j, c, slot):
         chip = plane * per_plane + j
@@ -189,7 +209,8 @@
 
     def fetch(i, carry):
         for g in range(2):
-            rad_copy(pair_at(i), g).start()
+            for q in range(QT):
+                rad_copy(pair_at(i), g, q).start()
         return carry
 
     lax.fori_loop(0, n_pair, fetch, 0)
@@ -233,10 +254,13 @@
 
     def aggregate(p):
         for g in range(2):
-            rad_copy(p, g).wait()
+            for q in range(QT):
+                rad_copy(p, g, q).wait()
             rays = jnp.dot(
                 hq[g],
-                rad[p, g].reshape(QT * GRP, 256),
+                jnp.concatenate(
+                    [rad[p, g, :, q * 256 : (q + 1) * 256] for q in range(QT)], axis=0
+                ),
                 preferred_element_type=jnp.float32,
             ).astype(jnp.bfloat16)
             for jj in range(2):
@@ -257,11 +281,11 @@
             def _():
                 pltpu.make_async_copy(send1.at[t], recv1.at[t], own_sem).start()
 
-    aggregate(my_pair)
+    aggregate(pair_at(0))
     for copy in w_copies:
         copy.wait()
     pl.semaphore_wait(barrier, n_space - 1 + n_dirs - 1)
-    dispatch(my_pair)
+    dispatch(pair_at(0))
     halo_copy(0).start()
     halo_copy(1).start()
     each_weight(lambda copy: copy.start())
@@ -393,19 +417,18 @@
                     s, g * ROWS : (g + 1) * ROWS, :
                 ]
         for g in range(2):
-            total = acc[g]
-            for q in range(QT):
-                start = 16 - q * HALF
-                late = jnp.concatenate(
-                    [padded[g, c, start : start + ROWS, :] for c in range(2)], axis=0
-                )
-                total = total + lax.dot_general(
-                    late,
-                    rad[p, g, q],
-                    (((1,), (1,)), ((), ())),
-                    preferred_element_type=jnp.float32,
-                )
-            acc[g] = total
+            for c in range(2):
+                for q in range(QT):
+                    start = 16 - q * HALF
+                    lhs[g, c * ROWS : (c + 1) * ROWS, q * 256 : (q + 1) * 256] = padded[
+                        g, c, start : start + ROWS, :
+                    ]
+            acc[g] = acc[g] + lax.dot_general(
+                lhs[g],
+                rad[p, g],
+                (((1,), (1,)), ((), ())),
+                preferred_element_type=jnp.float32,
+            )
         return carry
 
     lax.fori_loop(0, n_pair, project, 0)
@@ -482,7 +505,7 @@
             pltpu.VMEM((2, HB, TAPS * EXC, LANES), bf16),
             pltpu.VMEM((BLK + 2 * HB, TAPS + QT, EXC, LANES), f32),
             pltpu.VMEM(near_matrix.shape, bf16),
-            pltpu.VMEM((n_pair, 2, QT, GRP, 256), bf16),
+            pltpu.VMEM((n_pair, 2, GRP, QT * 256), bf16),
             pltpu.VMEM((weights.shape[1] // LANES, 2 * LIST, LANES), bf16),
             pltpu.VMEM((n_space, 2 * LIST, LANES), bf16),
             pltpu.VMEM((n_space, 2 * ROWS, LANES), bf16),
@@ -492,9 +515,10 @@
             pltpu.VMEM((n_space, 2 * ROWS, LANES), bf16),
             pltpu.VMEM((n_space, 2 * ROWS, LANES), bf16),
             pltpu.VMEM((2, 2, 16 + ROWS, 256), bf16),
+            pltpu.VMEM((2, 2 * ROWS, QT * 256), bf16),
             pltpu.VMEM((2, 2 * ROWS, GRP), f32),
             pltpu.SemaphoreType.DMA,
-            pltpu.SemaphoreType.DMA((n_pair, 2)),
+            pltpu.SemaphoreType.DMA((n_pair, 2, QT)),
             pltpu.SemaphoreType.DMA,
             pltpu.SemaphoreType.DMA((weights.shape[1] // LANES,)),
             pltpu.SemaphoreType.DMA((weights.shape[1] // LANES, 2)),

time: 75.5 us -> 73.4 us (0.972)
  the two profiles are of different devices: /device:TPU:1 before, /device:TPU:65 now
where the time goes in v8:
time: 73.4 us; the launch traced here: 73.3 us
  Pallas kernels  72.6 us (99%)
    pallas_call x1, Pallas kernels, local(): pl.pallas_call(functools.partial(kernel, n_space, n_dirs), out_shape=(jax...  70.7 us
    pallas_call x1, Pallas kernels, local(): pl.pallas_call(hand_out, out_shape=(jax.ShapeDtypeStruct(far.shape, bf16)...  1.87 us

profile of v8, /device:TPU:65, one launch (start us, length us, event | category | flops | bytes accessed | tf_op | source)
XLA Modules:
  0.0 73.3 jit_solution(4315458014970648228)
XLA Ops:
  0.6 70.7 %shard_map.95 = (bf16[32,8,1024]{2,1,0:T(8,128)(2,1)}, bf16[8,1024]{1,0:T(8,128)(2,1)}) custom-call(bf16[32,32,1024]{2,1,0:T(8,128)(2,1)} %hist_ref.1, bf16[4,2,512,2048]{3,2,1,0:T(8,128)(2,1)} %bitcast.4, bf16[8,8,128,128]{3,2,1,0:T(8,128)(2,1)} %mat_ref.1, bf16[16,512]{1,0:T(8,128)(2,1)} %bitcast.5, s32[8,8]{1,0:T(8,128)} %off_ref.1, s32[8,8]{1,0:T(8,128)} %del_ref.1, ...), custom_call_target="tpu_custom_call" | custom-call | flops 8589934592 | bytes 16777216 | tf_op jit(solution)/shard_map/pallas_call | solution.py:493
  71.4 1.9 %shard_map.96 = (bf16[32,8,1024]{2,1,0:T(8,128)(2,1)}, bf16[8,1024]{1,0:T(8,128)(2,1)}) custom-call(bf16[32,8,1024]{2,1,0:T(8,128)(2,1)} %get-tuple-element.6.far_ref, bf16[8,1024]{1,0:T(8,128)(2,1)} %get-tuple-element.7.near_ref), custom_call_target="tpu_custom_call" | custom-call | tf_op jit(solution)/shard_map/pallas_call | solution.py:555

commit v9 on v8

--- a/solution.py
+++ b/solution.py
@@ -16,9 +16,10 @@
 BLK = 8
 HB = 4
 EXC = 8
-HALF = EXC // 2
-ROWS = TAPS * HALF
-SPAN = ROWS + 16 * HALF
+PARTS = 4
+PAIR = EXC // PARTS
+ROWS = TAPS * PAIR
+SPAN = ROWS + 16 * PAIR
 GRP = 512
 
 
@@ -49,7 +50,8 @@
     wall,
     send1,
     recv1,
-    table,
+    table0,
+    table1,
     wtab,
     send2,
     recv2,
@@ -150,22 +152,22 @@
                 def _():
                     act(weight_copy(j, c, me))
 
-    def to_translator(t, slot):
+    def to_translator(t, slot, stage):
         return pltpu.make_async_remote_copy(
-            src_ref=send1.at[t],
-            dst_ref=recv1.at[slot],
-            send_sem=send1_sem.at[t],
-            recv_sem=recv1_sem.at[slot],
+            src_ref=send1.at[stage, t],
+            dst_ref=recv1.at[stage, slot],
+            send_sem=send1_sem.at[stage, t],
+            recv_sem=recv1_sem.at[stage, slot],
             device_id={"space": t},
             device_id_type=MESH,
         )
 
-    def to_owner(t, slot):
+    def to_owner(t, slot, stage):
         return pltpu.make_async_remote_copy(
-            src_ref=send2.at[t],
-            dst_ref=recv2.at[slot],
-            send_sem=send2_sem.at[t],
-            recv_sem=recv2_sem.at[slot],
+            src_ref=send2.at[stage, t],
+            dst_ref=recv2.at[stage, slot],
+            send_sem=send2_sem.at[stage, t],
+            recv_sem=recv2_sem.at[stage, slot],
             device_id={"space": t},
             device_id_type=MESH,
         )
@@ -239,18 +241,18 @@
         for g in range(2):
             for blk in range(BLK // 2):
                 for q in range(QT):
-                    taps = [ext[HB + g * (BLK // 2) + blk, 4 * i + q + a] for a in range(4)]
+                    taps = [ext[HB + g * (BLK // 2) + blk, 8 * i + q + a] for a in range(8)]
                     cols = q * GRP + blk * LANES
-                    for c in range(2):
-                        rows = [tap[c * HALF : (c + 1) * HALF] for tap in taps]
+                    for part in range(PARTS):
+                        rows = [tap[part * PAIR : (part + 1) * PAIR] for tap in taps]
                         hq[
                             g,
-                            pl.ds(pl.multiple_of(c * ROWS + i * 16, 16), 16),
+                            pl.ds(pl.multiple_of(part * ROWS + i * 16, 16), 16),
                             cols : cols + LANES,
                         ] = jnp.concatenate(rows, axis=0).astype(jnp.bfloat16)
         return carry
 
-    lax.fori_loop(0, TAPS // 4, stack, 0)
+    lax.fori_loop(0, TAPS // 8, stack, 0)
 
     def aggregate(p):
         for g in range(2):
@@ -264,28 +266,31 @@
                 preferred_element_type=jnp.float32,
             ).astype(jnp.bfloat16)
             for jj in range(2):
-                for c in range(2):
-                    send1[4 * p + 2 * jj + c, pl.ds(g * ROWS, ROWS), :] = rays[
-                        c * ROWS : (c + 1) * ROWS, jj * LANES : (jj + 1) * LANES
+                for part in range(PARTS):
+                    c, stage = part // 2, part % 2
+                    send1[stage, 4 * p + 2 * jj + c, pl.ds(g * ROWS, ROWS), :] = rays[
+                        part * ROWS : (part + 1) * ROWS, jj * LANES : (jj + 1) * LANES
                     ]
 
-    def dispatch(p):
+    def dispatch(p, stage):
         for j in range(4):
             t = target(p, j)
 
             @pl.when(t != me)
             def _():
-                to_translator(t, me).start()
+                to_translator(t, me, stage).start()
 
             @pl.when(t == me)
             def _():
-                pltpu.make_async_copy(send1.at[t], recv1.at[t], own_sem).start()
+                pltpu.make_async_copy(
+                    send1.at[stage, t], recv1.at[stage, t], own_sem.at[stage]
+                ).start()
 
     aggregate(pair_at(0))
     for copy in w_copies:
         copy.wait()
     pl.semaphore_wait(barrier, n_space - 1 + n_dirs - 1)
-    dispatch(pair_at(0))
+    dispatch(pair_at(0), 0)
     halo_copy(0).start()
     halo_copy(1).start()
     each_weight(lambda copy: copy.start())
@@ -297,10 +302,16 @@
     def agg_step(i, carry):
         p = pair_at(i)
         aggregate(p)
-        dispatch(p)
+        dispatch(p, 0)
         return carry
 
     lax.fori_loop(1, n_pair, agg_step, 0)
+
+    def second_stage(i, carry):
+        dispatch(pair_at(i), 1)
+        return carry
+
+    lax.fori_loop(0, n_pair, second_stage, 0)
 
     @pl.when(plane == home)
     def _():
@@ -314,62 +325,73 @@
         for i in range(1, n_dirs):
             weights_up(lax.rem(plane + i, n_dirs)).start()
 
-    table[:, ROWS:SPAN, :] = jnp.zeros((table.shape[0], SPAN - ROWS, LANES), jnp.float32)
+    for table in (table0, table1):
+        table[:, ROWS:SPAN, :] = jnp.zeros((table.shape[0], SPAN - ROWS, LANES), jnp.float32)
     acc[...] = jnp.zeros_like(acc)
-    padded[:, :, 0:16, :] = jnp.zeros((2, 2, 16, 256), jnp.bfloat16)
-
-    def take_in(i, carry):
-        p = pair_from(i)
-        for j in range(4):
-            s = 4 * p + j
-
-            @pl.when(s != me)
-            def _():
-                to_translator(s, s).wait_recv()
-
-            @pl.when(s == me)
-            def _():
-                pltpu.make_async_copy(send1.at[s], recv1.at[s], own_sem).wait()
-
-            for g in range(2):
-                table[2 * s + g, 0:ROWS, :] = recv1[s, g * ROWS : (g + 1) * ROWS, :].astype(
-                    jnp.float32
-                )
-        return carry
+    padded[:, :, 0:16, :] = jnp.zeros((2, PARTS, 16, 256), jnp.bfloat16)
+
+    def take_in(stage, table):
+        def step(i, carry):
+            p = pair_from(i)
+            for j in range(4):
+                s = 4 * p + j
+
+                @pl.when(s != me)
+                def _():
+                    to_translator(s, s, stage).wait_recv()
+
+                @pl.when(s == me)
+                def _():
+                    pltpu.make_async_copy(
+                        send1.at[stage, s], recv1.at[stage, s], own_sem.at[stage]
+                    ).wait()
+
+                for g in range(2):
+                    table[2 * s + g, 0:ROWS, :] = recv1[
+                        stage, s, g * ROWS : (g + 1) * ROWS, :
+                    ].astype(jnp.float32)
+            return carry
+
+        lax.fori_loop(0, n_pair, step, 0)
+
+    def translate(stage, table):
+        def step(i, carry):
+            p = pair_at(i)
+            for j in range(4):
+                t = target(p, j)
+                for g in range(2):
+                    weights = wtab[t, g * LIST : (g + 1) * LIST, :]
+                    total = jnp.zeros((ROWS, LANES), jnp.float32)
+                    for slot in range(LIST):
+                        first = lag_ref[slot, 2 * t + g] * PAIR
+                        tile = table[src_ref[slot, 2 * t + g], pl.ds(first, ROWS), :]
+                        total = total + weights[slot : slot + 1, :] * tile
+                    send2[stage, t, g * ROWS : (g + 1) * ROWS, :] = total.astype(jnp.bfloat16)
+
+                @pl.when(t != me)
+                def _():
+                    to_owner(t, me, stage).start()
+
+                @pl.when(t == me)
+                def _():
+                    pltpu.make_async_copy(
+                        send2.at[stage, t], recv2.at[stage, t], own_sem.at[stage]
+                    ).start()
+
+            return carry
+
+        lax.fori_loop(0, n_pair, step, 0)
+
+    take_in(0, table0)
 
     @pl.when(plane != home)
     def _():
         weights_up(home).wait_recv()
 
     wtab[...] = wall[...].astype(jnp.float32)
-    lax.fori_loop(0, n_pair, take_in, 0)
-
-    def translate(i, carry):
-        p = pair_at(i)
-        for j in range(4):
-            t = target(p, j)
-            for g in range(2):
-                weights = wtab[t, g * LIST : (g + 1) * LIST, :]
-                total = jnp.zeros((ROWS, LANES), jnp.float32)
-                for slot in range(LIST):
-                    first = lag_ref[slot, 2 * t + g] * HALF
-                    total = (
-                        total
-                        + weights[slot : slot + 1, :] * table[src_ref[slot, 2 * t + g], pl.ds(first, ROWS), :]
-                    )
-                send2[t, g * ROWS : (g + 1) * ROWS, :] = total.astype(jnp.bfloat16)
-
-            @pl.when(t != me)
-            def _():
-                to_owner(t, me).start()
-
-            @pl.when(t == me)
-            def _():
-                pltpu.make_async_copy(send2.at[t], recv2.at[t], own_sem).start()
-
-        return carry
-
-    lax.fori_loop(0, n_pair, translate, 0)
+    translate(0, table0)
+    take_in(1, table1)
+    translate(1, table1)
 
     for side in range(2):
         halo_copy(side).wait_recv()
@@ -402,26 +424,29 @@
         p = pair_from(i)
         for j in range(4):
             s = 4 * p + j
-
-            @pl.when(s != me)
-            def _():
-                to_owner(s, s).wait_recv()
-
-            @pl.when(s == me)
-            def _():
-                pltpu.make_async_copy(send2.at[s], recv2.at[s], own_sem).wait()
-
             jj, c = j // 2, j % 2
-            for g in range(2):
-                padded[g, c, 16 : 16 + ROWS, jj * LANES : (jj + 1) * LANES] = recv2[
-                    s, g * ROWS : (g + 1) * ROWS, :
-                ]
+            for stage in range(2):
+
+                @pl.when(s != me)
+                def _():
+                    to_owner(s, s, stage).wait_recv()
+
+                @pl.when(s == me)
+                def _():
+                    pltpu.make_async_copy(
+                        send2.at[stage, s], recv2.at[stage, s], own_sem.at[stage]
+                    ).wait()
+
+                for g in range(2):
+                    padded[g, 2 * c + stage, 16 : 16 + ROWS, jj * LANES : (jj + 1) * LANES] = (
+                        recv2[stage, s, g * ROWS : (g + 1) * ROWS, :]
+                    )
         for g in range(2):
-            for c in range(2):
+            for part in range(PARTS):
                 for q in range(QT):
-                    start = 16 - q * HALF
-                    lhs[g, c * ROWS : (c + 1) * ROWS, q * 256 : (q + 1) * 256] = padded[
-                        g, c, start : start + ROWS, :
+                    start = 16 - q * PAIR
+                    lhs[g, part * ROWS : (part + 1) * ROWS, q * 256 : (q + 1) * 256] = padded[
+                        g, part, start : start + ROWS, :
                     ]
             acc[g] = acc[g] + lax.dot_general(
                 lhs[g],
@@ -435,22 +460,24 @@
 
     def finish(a, carry):
         for g in range(2):
-            halves = [
-                acc[g, pl.ds(c * ROWS + a * 2 * HALF, 2 * HALF), :] for c in range(2)
+            parts = [
+                acc[g, pl.ds(pl.multiple_of(part * ROWS + a * 8, 8), 8), :]
+                for part in range(PARTS)
             ]
-            for i in range(2):
-                rows = [half[i * HALF : (i + 1) * HALF] for half in halves]
-                far_ref[2 * a + i, :, g * GRP : (g + 1) * GRP] = jnp.concatenate(
+            for i in range(4):
+                rows = [part[i * PAIR : (i + 1) * PAIR] for part in parts]
+                far_ref[4 * a + i, :, g * GRP : (g + 1) * GRP] = jnp.concatenate(
                     rows, axis=0
                 ).astype(jnp.bfloat16)
         return carry
 
-    lax.fori_loop(0, TAPS // 2, finish, 0)
+    lax.fori_loop(0, TAPS // 4, finish, 0)
 
     def drain(i, carry):
         t = lax.rem(me + i, n_space)
-        to_translator(t, me).wait_send()
-        to_owner(t, me).wait_send()
+        for stage in range(2):
+            to_translator(t, me, stage).wait_send()
+            to_owner(t, me, stage).wait_send()
         return carry
 
     lax.fori_loop(1, n_space, drain, 0)
@@ -500,7 +527,7 @@
         out_specs=(vmem, vmem),
         scratch_shapes=[
             pltpu.VMEM((TAPS, 2 * EXC, cur), bf16),
-            pltpu.VMEM((2, 2 * ROWS, QT * GRP), bf16),
+            pltpu.VMEM((2, PARTS * ROWS, QT * GRP), bf16),
             pltpu.VMEM((BLK, TAPS * EXC, LANES), bf16),
             pltpu.VMEM((2, HB, TAPS * EXC, LANES), bf16),
             pltpu.VMEM((BLK + 2 * HB, TAPS + QT, EXC, LANES), f32),
@@ -508,15 +535,16 @@
             pltpu.VMEM((n_pair, 2, GRP, QT * 256), bf16),
             pltpu.VMEM((weights.shape[1] // LANES, 2 * LIST, LANES), bf16),
             pltpu.VMEM((n_space, 2 * LIST, LANES), bf16),
-            pltpu.VMEM((n_space, 2 * ROWS, LANES), bf16),
-            pltpu.VMEM((n_space, 2 * ROWS, LANES), bf16),
+            pltpu.VMEM((2, n_space, 2 * ROWS, LANES), bf16),
+            pltpu.VMEM((2, n_space, 2 * ROWS, LANES), bf16),
+            pltpu.VMEM((2 * n_space, SPAN, LANES), f32),
             pltpu.VMEM((2 * n_space, SPAN, LANES), f32),
             pltpu.VMEM((n_space, 2 * LIST, LANES), f32),
-            pltpu.VMEM((n_space, 2 * ROWS, LANES), bf16),
-            pltpu.VMEM((n_space, 2 * ROWS, LANES), bf16),
-            pltpu.VMEM((2, 2, 16 + ROWS, 256), bf16),
-            pltpu.VMEM((2, 2 * ROWS, QT * 256), bf16),
-            pltpu.VMEM((2, 2 * ROWS, GRP), f32),
+            pltpu.VMEM((2, n_space, 2 * ROWS, LANES), bf16),
+            pltpu.VMEM((2, n_space, 2 * ROWS, LANES), bf16),
+            pltpu.VMEM((2, PARTS, 16 + ROWS, 256), bf16),
+            pltpu.VMEM((2, PARTS * ROWS, QT * 256), bf16),
+            pltpu.VMEM((2, PARTS * ROWS, GRP), f32),
             pltpu.SemaphoreType.DMA,
             pltpu.SemaphoreType.DMA((n_pair, 2, QT)),
             pltpu.SemaphoreType.DMA,
@@ -528,11 +556,11 @@
             pltpu.SemaphoreType.DMA,
             pltpu.SemaphoreType.DMA((2,)),
             pltpu.SemaphoreType.DMA((2,)),
-            pltpu.SemaphoreType.DMA,
-            pltpu.SemaphoreType.DMA((n_space,)),
-            pltpu.SemaphoreType.DMA((n_space,)),
-            pltpu.SemaphoreType.DMA((n_space,)),
-            pltpu.SemaphoreType.DMA((n_space,)),
+            pltpu.SemaphoreType.DMA((2,)),
+            pltpu.SemaphoreType.DMA((2, n_space)),
+            pltpu.SemaphoreType.DMA((2, n_space)),
+            pltpu.SemaphoreType.DMA((2, n_space)),
+            pltpu.SemaphoreType.DMA((2, n_space)),
         ],
         compiler_params=pltpu.CompilerParams(
             collective_id=0, has_side_effects=True, vmem_limit_bytes=56 * 1024 * 1024

time: 73.4 us -> 71.6 us (0.975)
  the two profiles are of different devices: /device:TPU:65 before, /device:TPU:1 now
where the time goes in v9:
time: 71.6 us; the launch traced here: 71 us
  Pallas kernels  70.3 us (98%)
    pallas_call x1, Pallas kernels, local(): pl.pallas_call(functools.partial(kernel, n_space, n_dirs), out_shape=(jax...  68.5 us
    pallas_call x1, Pallas kernels, local(): pl.pallas_call(hand_out, out_shape=(jax.ShapeDtypeStruct(far.shape, bf16)...  1.87 us

profile of v9, /device:TPU:1, one launch (start us, length us, event | category | flops | bytes accessed | tf_op | source)
XLA Modules:
  0.0 71.0 jit_solution(15918801842359849015)
XLA Ops:
  0.6 68.5 %shard_map.95 = (bf16[32,8,1024]{2,1,0:T(8,128)(2,1)}, bf16[8,1024]{1,0:T(8,128)(2,1)}) custom-call(bf16[32,32,1024]{2,1,0:T(8,128)(2,1)} %hist_ref.1, bf16[4,2,512,2048]{3,2,1,0:T(8,128)(2,1)} %bitcast.4, bf16[8,8,128,128]{3,2,1,0:T(8,128)(2,1)} %mat_ref.1, bf16[16,512]{1,0:T(8,128)(2,1)} %bitcast.5, s32[8,8]{1,0:T(8,128)} %off_ref.1, s32[8,8]{1,0:T(8,128)} %del_ref.1, ...), custom_call_target="tpu_custom_call" | custom-call | flops 8589934592 | bytes 16777216 | tf_op jit(solution)/shard_map/pallas_call | solution.py:520
  69.1 1.9 %shard_map.96 = (bf16[32,8,1024]{2,1,0:T(8,128)(2,1)}, bf16[8,1024]{1,0:T(8,128)(2,1)}) custom-call(bf16[32,8,1024]{2,1,0:T(8,128)(2,1)} %get-tuple-element.6.far_ref, bf16[8,1024]{1,0:T(8,128)(2,1)} %get-tuple-element.7.near_ref), custom_call_target="tpu_custom_call" | custom-call | tf_op jit(solution)/shard_map/pallas_call | solution.py:583

commit v10 on v9

--- a/solution.py
+++ b/solution.py
@@ -156,7 +156,7 @@
         return pltpu.make_async_remote_copy(
             src_ref=send1.at[stage, t],
             dst_ref=recv1.at[stage, slot],
-            send_sem=send1_sem.at[stage, t],
+            send_sem=send1_sem.at[stage],
             recv_sem=recv1_sem.at[stage, slot],
             device_id={"space": t},
             device_id_type=MESH,
@@ -166,11 +166,22 @@
         return pltpu.make_async_remote_copy(
             src_ref=send2.at[stage, t],
             dst_ref=recv2.at[stage, slot],
-            send_sem=send2_sem.at[stage, t],
+            send_sem=send2_sem.at[stage],
             recv_sem=recv2_sem.at[stage, slot],
             device_id={"space": t},
             device_id_type=MESH,
         )
+
+    def all_sent(send, recv, sem, stage):
+        most = pl.ds(0, n_space - 1)
+        pltpu.make_async_remote_copy(
+            src_ref=send.at[stage, most],
+            dst_ref=recv.at[stage, most],
+            send_sem=sem.at[stage],
+            recv_sem=sem.at[stage],
+            device_id={"space": right},
+            device_id_type=MESH,
+        ).wait_send()
 
     def halo_copy(side):
         return pltpu.make_async_remote_copy(
@@ -272,8 +283,8 @@
                         part * ROWS : (part + 1) * ROWS, jj * LANES : (jj + 1) * LANES
                     ]
 
-    def dispatch(p, stage):
-        for j in range(4):
+    def dispatch(pairs, stage):
+        for j, p in [(j, p) for j in range(4) for p in pairs]:
             t = target(p, j)
 
             @pl.when(t != me)
@@ -290,7 +301,7 @@
     for copy in w_copies:
         copy.wait()
     pl.semaphore_wait(barrier, n_space - 1 + n_dirs - 1)
-    dispatch(pair_at(0), 0)
+    dispatch([pair_at(0)], 0)
     halo_copy(0).start()
     halo_copy(1).start()
     each_weight(lambda copy: copy.start())
@@ -302,16 +313,16 @@
     def agg_step(i, carry):
         p = pair_at(i)
         aggregate(p)
-        dispatch(p, 0)
+        dispatch([p], 0)
         return carry
 
     lax.fori_loop(1, n_pair, agg_step, 0)
 
     def second_stage(i, carry):
-        dispatch(pair_at(i), 1)
-        return carry
-
-    lax.fori_loop(0, n_pair, second_stage, 0)
+        dispatch([pair_at(2 * i), pair_at(2 * i + 1)], 1)
+        return carry
+
+    lax.fori_loop(0, n_pair // 2, second_stage, 0)
 
     @pl.when(plane == home)
     def _():
@@ -419,6 +430,18 @@
                 preferred_element_type=jnp.float32,
             )
         near_ref[:, b * LANES : (b + 1) * LANES] = near.astype(jnp.bfloat16)
+
+    each_weight(lambda copy: copy.wait_send())
+
+    @pl.when(plane == home)
+    def _():
+        for i in range(1, n_dirs):
+            weights_up(lax.rem(plane + i, n_dirs)).wait_send()
+
+    for side in range(2):
+        halo_copy(side).wait_send()
+    for stage in range(2):
+        all_sent(send1, recv1, send1_sem, stage)
 
     def project(i, carry):
         p = pair_from(i)
@@ -472,24 +495,8 @@
         return carry
 
     lax.fori_loop(0, TAPS // 4, finish, 0)
-
-    def drain(i, carry):
-        t = lax.rem(me + i, n_space)
-        for stage in range(2):
-            to_translator(t, me, stage).wait_send()
-            to_owner(t, me, stage).wait_send()
-        return carry
-
-    lax.fori_loop(1, n_space, drain, 0)
-    each_weight(lambda copy: copy.wait_send())
-
-    @pl.when(plane == home)
-    def _():
-        for i in range(1, n_dirs):
-            weights_up(lax.rem(plane + i, n_dirs)).wait_send()
-
-    for side in range(2):
-        halo_copy(side).wait_send()
+    for stage in range(2):
+        all_sent(send2, recv2, send2_sem, stage)
 
 
 def hand_out(far_ref, near_ref, far_out, near_out):
@@ -557,9 +564,9 @@
             pltpu.SemaphoreType.DMA((2,)),
             pltpu.SemaphoreType.DMA((2,)),
             pltpu.SemaphoreType.DMA((2,)),
+            pltpu.SemaphoreType.DMA((2,)),
             pltpu.SemaphoreType.DMA((2, n_space)),
-            pltpu.SemaphoreType.DMA((2, n_space)),
-            pltpu.SemaphoreType.DMA((2, n_space)),
+            pltpu.SemaphoreType.DMA((2,)),
             pltpu.SemaphoreType.DMA((2, n_space)),
         ],
         compiler_params=pltpu.CompilerParams(

time: 71.6 us -> 70 us (0.978)
  Pallas kernels: 70.3 us -> 68.8 us
    pallas_call x1, Pallas kernels: 68.5 us -> 66.9 us  [local(): pl.pallas_call(functools.partial(kernel, n_space, n_dirs), out_shape=(jax...]
where the time goes in v10:
time: 70 us; the launch traced here: 69.4 us
  Pallas kernels  68.8 us (98%)
    pallas_call x1, Pallas kernels, local(): pl.pallas_call(functools.partial(kernel, n_space, n_dirs), out_shape=(jax...  66.9 us
    pallas_call x1, Pallas kernels, local(): pl.pallas_call(hand_out, out_shape=(jax.ShapeDtypeStruct(far.shape, bf16)...  1.87 us

profile of v10, /device:TPU:1, one launch (start us, length us, event | category | flops | bytes accessed | tf_op | source)
XLA Modules:
  0.0 69.4 jit_solution(686448184220494827)
XLA Ops:
  0.6 66.9 %shard_map.95 = (bf16[32,8,1024]{2,1,0:T(8,128)(2,1)}, bf16[8,1024]{1,0:T(8,128)(2,1)}) custom-call(bf16[32,32,1024]{2,1,0:T(8,128)(2,1)} %hist_ref.1, bf16[4,2,512,2048]{3,2,1,0:T(8,128)(2,1)} %bitcast.4, bf16[8,8,128,128]{3,2,1,0:T(8,128)(2,1)} %mat_ref.1, bf16[16,512]{1,0:T(8,128)(2,1)} %bitcast.5, s32[8,8]{1,0:T(8,128)} %off_ref.1, s32[8,8]{1,0:T(8,128)} %del_ref.1, ...), custom_call_target="tpu_custom_call" | custom-call | flops 8589934592 | bytes 16777216 | tf_op jit(solution)/shard_map/pallas_call | solution.py:527
  67.6 1.9 %shard_map.96 = (bf16[32,8,1024]{2,1,0:T(8,128)(2,1)}, bf16[8,1024]{1,0:T(8,128)(2,1)}) custom-call(bf16[32,8,1024]{2,1,0:T(8,128)(2,1)} %get-tuple-element.6.far_ref, bf16[8,1024]{1,0:T(8,128)(2,1)} %get-tuple-element.7.near_ref), custom_call_target="tpu_custom_call" | custom-call | tf_op jit(solution)/shard_map/pallas_call | solution.py:590

commit v11 on v10

--- a/solution.py
+++ b/solution.py
@@ -100,8 +100,8 @@
         return pair_of(dy + my_core * (SIDE - 2 * dy), other)
 
     def pair_from(i):
-        dy, other = step_of(lax.rem(i + 2, n_pair))
-        return pair_of(dy, other)
+        dy = jnp.where(i < 4, 2 * lax.rem(i, 2), 3 - 2 * lax.rem(i, 2))
+        return pair_of(dy, lax.rem(lax.div(i, 2), 2))
 
     def target(p, j):
         own = lax.rem(p, 2) == lax.div(my_x, 2)
@@ -302,27 +302,31 @@
         copy.wait()
     pl.semaphore_wait(barrier, n_space - 1 + n_dirs - 1)
     dispatch([pair_at(0)], 0)
-    halo_copy(0).start()
-    halo_copy(1).start()
     each_weight(lambda copy: copy.start())
 
     @pl.when(plane == home)
     def _():
         own_weights.start()
 
+    aggregate(pair_at(1))
+    dispatch([pair_at(1)], 0)
+
     def agg_step(i, carry):
-        p = pair_at(i)
-        aggregate(p)
-        dispatch([p], 0)
-        return carry
-
-    lax.fori_loop(1, n_pair, agg_step, 0)
+        pairs = [pair_at(2 * i), pair_at(2 * i + 1)]
+        for p in pairs:
+            aggregate(p)
+        dispatch(pairs, 0)
+        return carry
+
+    lax.fori_loop(1, n_pair // 2, agg_step, 0)
 
     def second_stage(i, carry):
         dispatch([pair_at(2 * i), pair_at(2 * i + 1)], 1)
         return carry
 
     lax.fori_loop(0, n_pair // 2, second_stage, 0)
+    halo_copy(0).start()
+    halo_copy(1).start()
 
     @pl.when(plane == home)
     def _():
@@ -367,8 +371,8 @@
 
     def translate(stage, table):
         def step(i, carry):
-            p = pair_at(i)
-            for j in range(4):
+            pairs = [pair_at(2 * i), pair_at(2 * i + 1)]
+            for j, p in [(j, p) for j in range(4) for p in pairs]:
                 t = target(p, j)
                 for g in range(2):
                     weights = wtab[t, g * LIST : (g + 1) * LIST, :]
@@ -391,7 +395,7 @@
 
             return carry
 
-        lax.fori_loop(0, n_pair, step, 0)
+        lax.fori_loop(0, n_pair // 2, step, 0)
 
     take_in(0, table0)
 
@@ -499,9 +503,19 @@
         all_sent(send2, recv2, send2_sem, stage)
 
 
-def hand_out(far_ref, near_ref, far_out, near_out):
-    far_out[...] = far_ref[...]
-    near_out[...] = near_ref[...]
+def hand_out(far_ref, near_ref, far_out, near_out, far, near, in_sem, out_sem):
+    pieces = [pl.ds(i * 8, 8) for i in range(TAPS // 8)]
+    views = [(far_ref.at[at], far.at[at], far_out.at[at]) for at in pieces]
+    views.append((near_ref, near, near_out))
+    reads = [pltpu.make_async_copy(v[0], v[1], in_sem.at[i]) for i, v in enumerate(views)]
+    writes = [pltpu.make_async_copy(v[1], v[2], out_sem.at[i]) for i, v in enumerate(views)]
+    for read in reads:
+        read.start()
+    for read, write in zip(reads, writes):
+        read.wait()
+        write.start()
+    for write in writes:
+        write.wait()
 
 
 def local(
@@ -593,8 +607,14 @@
             jax.ShapeDtypeStruct(far.shape, bf16),
             jax.ShapeDtypeStruct(near.shape, bf16),
         ),
-        in_specs=[vmem] * 2,
-        out_specs=(vmem, vmem),
+        in_specs=[any_spec] * 2,
+        out_specs=(any_spec, any_spec),
+        scratch_shapes=[
+            pltpu.VMEM(far.shape, bf16),
+            pltpu.VMEM(near.shape, bf16),
+            pltpu.SemaphoreType.DMA((TAPS // 8 + 1,)),
+            pltpu.SemaphoreType.DMA((TAPS // 8 + 1,)),
+        ],
         compiler_params=pltpu.CompilerParams(vmem_limit_bytes=56 * 1024 * 1024),
     )(far, near)
     return near, far

time: 70 us -> 73.1 us (1.044)
  Pallas kernels: 68.8 us -> 72.1 us
    pallas_call x1, Pallas kernels: 66.9 us -> 70.2 us  [local(): pl.pallas_call(functools.partial(kernel, n_space, n_dirs), out_shape=(jax...]
where the time goes in v11:
time: 73.1 us; the launch traced here: 72.7 us
  Pallas kernels  72.1 us (99%)
    pallas_call x1, Pallas kernels, local(): pl.pallas_call(functools.partial(kernel, n_space, n_dirs), out_shape=(jax...  70.2 us
    pallas_call x1, Pallas kernels, local(): pl.pallas_call(hand_out, out_shape=(jax.ShapeDtypeStruct(far.shape, bf16)...  1.84 us

profile of v11, /device:TPU:1, one launch (start us, length us, event | category | flops | bytes accessed | tf_op | source)
XLA Modules:
  0.0 72.7 jit_solution(13827664602048724070)
XLA Ops:
  0.6 70.2 %shard_map.95 = (bf16[32,8,1024]{2,1,0:T(8,128)(2,1)}, bf16[8,1024]{1,0:T(8,128)(2,1)}) custom-call(bf16[32,32,1024]{2,1,0:T(8,128)(2,1)} %hist_ref.1, bf16[4,2,512,2048]{3,2,1,0:T(8,128)(2,1)} %bitcast.4, bf16[8,8,128,128]{3,2,1,0:T(8,128)(2,1)} %mat_ref.1, bf16[16,512]{1,0:T(8,128)(2,1)} %bitcast.5, s32[8,8]{1,0:T(8,128)} %off_ref.1, s32[8,8]{1,0:T(8,128)} %del_ref.1, ...), custom_call_target="tpu_custom_call" | custom-call | flops 8589934592 | bytes 16777216 | tf_op jit(solution)/shard_map/pallas_call | solution.py:541
  70.9 1.8 %shard_map.96 = (bf16[32,8,1024]{2,1,0:T(8,128)(2,1)}, bf16[8,1024]{1,0:T(8,128)(2,1)}) custom-call(bf16[32,8,1024]{2,1,0:T(8,128)(2,1)} %get-tuple-element.6.far_ref, bf16[8,1024]{1,0:T(8,128)(2,1)} %get-tuple-element.7.near_ref), custom_call_target="tpu_custom_call" | custom-call | tf_op jit(solution)/shard_map/pallas_call | solution.py:604

commit v12 on v10

--- a/solution.py
+++ b/solution.py
@@ -283,8 +283,8 @@
                         part * ROWS : (part + 1) * ROWS, jj * LANES : (jj + 1) * LANES
                     ]
 
-    def dispatch(pairs, stage):
-        for j, p in [(j, p) for j in range(4) for p in pairs]:
+    def dispatch(p, stage):
+        for j in range(4):
             t = target(p, j)
 
             @pl.when(t != me)
@@ -301,7 +301,7 @@
     for copy in w_copies:
         copy.wait()
     pl.semaphore_wait(barrier, n_space - 1 + n_dirs - 1)
-    dispatch([pair_at(0)], 0)
+    dispatch(pair_at(0), 0)
     halo_copy(0).start()
     halo_copy(1).start()
     each_weight(lambda copy: copy.start())
@@ -313,16 +313,16 @@
     def agg_step(i, carry):
         p = pair_at(i)
         aggregate(p)
-        dispatch([p], 0)
+        dispatch(p, 0)
         return carry
 
     lax.fori_loop(1, n_pair, agg_step, 0)
 
     def second_stage(i, carry):
-        dispatch([pair_at(2 * i), pair_at(2 * i + 1)], 1)
-        return carry
-
-    lax.fori_loop(0, n_pair // 2, second_stage, 0)
+        dispatch(pair_at(i), 1)
+        return carry
+
+    lax.fori_loop(0, n_pair, second_stage, 0)
 
     @pl.when(plane == home)
     def _():

time: 70 us -> 70.1 us (level)
  no operation moved by 1% of the time
where the time goes in v12:
time: 70.1 us; the launch traced here: 69.4 us
  Pallas kernels  68.8 us (98%)
    pallas_call x1, Pallas kernels, local(): pl.pallas_call(functools.partial(kernel, n_space, n_dirs), out_shape=(jax...  66.9 us
    pallas_call x1, Pallas kernels, local(): pl.pallas_call(hand_out, out_shape=(jax.ShapeDtypeStruct(far.shape, bf16)...  1.87 us

profile of v12, /device:TPU:1, one launch (start us, length us, event | category | flops | bytes accessed | tf_op | source)
XLA Modules:
  0.0 69.4 jit_solution(13270528280365846091)
XLA Ops:
  0.6 66.9 %shard_map.95 = (bf16[32,8,1024]{2,1,0:T(8,128)(2,1)}, bf16[8,1024]{1,0:T(8,128)(2,1)}) custom-call(bf16[32,32,1024]{2,1,0:T(8,128)(2,1)} %hist_ref.1, bf16[4,2,512,2048]{3,2,1,0:T(8,128)(2,1)} %bitcast.4, bf16[8,8,128,128]{3,2,1,0:T(8,128)(2,1)} %mat_ref.1, bf16[16,512]{1,0:T(8,128)(2,1)} %bitcast.5, s32[8,8]{1,0:T(8,128)} %off_ref.1, s32[8,8]{1,0:T(8,128)} %del_ref.1, ...), custom_call_target="tpu_custom_call" | custom-call | flops 8589934592 | bytes 16777216 | tf_op jit(solution)/shard_map/pallas_call | solution.py:527
  67.6 1.9 %shard_map.96 = (bf16[32,8,1024]{2,1,0:T(8,128)(2,1)}, bf16[8,1024]{1,0:T(8,128)(2,1)}) custom-call(bf16[32,8,1024]{2,1,0:T(8,128)(2,1)} %get-tuple-element.6.far_ref, bf16[8,1024]{1,0:T(8,128)(2,1)} %get-tuple-element.7.near_ref), custom_call_target="tpu_custom_call" | custom-call | tf_op jit(solution)/shard_map/pallas_call | solution.py:590

commit v13 on v10

--- a/solution.py
+++ b/solution.py
@@ -100,8 +100,8 @@
         return pair_of(dy + my_core * (SIDE - 2 * dy), other)
 
     def pair_from(i):
-        dy, other = step_of(lax.rem(i + 2, n_pair))
-        return pair_of(dy, other)
+        dy = jnp.where(i < 4, 2 * lax.rem(i, 2), 3 - 2 * lax.rem(i, 2))
+        return pair_of(dy, lax.rem(lax.div(i, 2), 2))
 
     def target(p, j):
         own = lax.rem(p, 2) == lax.div(my_x, 2)
@@ -401,9 +401,6 @@
 
     wtab[...] = wall[...].astype(jnp.float32)
     translate(0, table0)
-    take_in(1, table1)
-    translate(1, table1)
-
     for side in range(2):
         halo_copy(side).wait_recv()
 
@@ -430,6 +427,9 @@
                 preferred_element_type=jnp.float32,
             )
         near_ref[:, b * LANES : (b + 1) * LANES] = near.astype(jnp.bfloat16)
+
+    take_in(1, table1)
+    translate(1, table1)
 
     each_weight(lambda copy: copy.wait_send())
 

time: 70 us -> 70 us (level)
  no operation moved by 1% of the time
where the time goes in v13:
time: 70 us; the launch traced here: 69.4 us
  Pallas kernels  68.8 us (98%)
    pallas_call x1, Pallas kernels, local(): pl.pallas_call(functools.partial(kernel, n_space, n_dirs), out_shape=(jax...  66.9 us
    pallas_call x1, Pallas kernels, local(): pl.pallas_call(hand_out, out_shape=(jax.ShapeDtypeStruct(far.shape, bf16)...  1.87 us

profile of v13, /device:TPU:1, one launch (start us, length us, event | category | flops | bytes accessed | tf_op | source)
XLA Modules:
  0.0 69.4 jit_solution(2107052584909000115)
XLA Ops:
  0.6 66.9 %shard_map.95 = (bf16[32,8,1024]{2,1,0:T(8,128)(2,1)}, bf16[8,1024]{1,0:T(8,128)(2,1)}) custom-call(bf16[32,32,1024]{2,1,0:T(8,128)(2,1)} %hist_ref.1, bf16[4,2,512,2048]{3,2,1,0:T(8,128)(2,1)} %bitcast.4, bf16[8,8,128,128]{3,2,1,0:T(8,128)(2,1)} %mat_ref.1, bf16[16,512]{1,0:T(8,128)(2,1)} %bitcast.5, s32[8,8]{1,0:T(8,128)} %off_ref.1, s32[8,8]{1,0:T(8,128)} %del_ref.1, ...), custom_call_target="tpu_custom_call" | custom-call | flops 8589934592 | bytes 16777216 | tf_op jit(solution)/shard_map/pallas_call | solution.py:527
  67.5 1.9 %shard_map.96 = (bf16[32,8,1024]{2,1,0:T(8,128)(2,1)}, bf16[8,1024]{1,0:T(8,128)(2,1)}) custom-call(bf16[32,8,1024]{2,1,0:T(8,128)(2,1)} %get-tuple-element.6.far_ref, bf16[8,1024]{1,0:T(8,128)(2,1)} %get-tuple-element.7.near_ref), custom_call_target="tpu_custom_call" | custom-call | tf_op jit(solution)/shard_map/pallas_call | solution.py:590
